TPU v7x, 256 devices: a whole 4x4x8 slice. The times are simulated.
256 devices in a mesh: gx: 4 (over z_lo), gy: 4 (over z_hi, core), gz: 16 (over y, x).
Axes of the slice: x: 4, y: 4, z: 8 (z_hi: 2, z_lo: 4; z = z_hi * 4 + z_lo), core: 2. Of those that a mesh axis runs over, the one named last changes fastest.
Arguments:
- features: bfloat16 [262144, 128], P(('gx', 'gy', 'gz')), may hold values from -6 to 6
- up_weight: bfloat16 [128, 128], replicated, may hold values from -0.5 to 0.5
- radial_weight: bfloat16 [8, 384], replicated, may hold values from -2 to 2
- out_weight: bfloat16 [384, 128], replicated, may hold values from -0.3125 to 0.3125
- read_weight: float32 [4, 128], replicated, may hold values from -0.5 to 0.5
- ghost_rows: int32 [8, 8, 32, 32], P('gx', 'gy', 'gz'), may hold values from 0 to 1023, as said below
- senders: int32 [32, 262144], P(None, ('gx', 'gy', 'gz')), may hold values from 0 to 3071, as said below
- live: int32 [32, 262144], P(None, ('gx', 'gy', 'gz')), may hold values from 0 to 1, as said below
- harmonics: bfloat16 [9, 32, 262144], P(None, None, ('gx', 'gy', 'gz')), may hold values from -6 to 6
- radial: bfloat16 [8, 32, 262144], P(None, None, ('gx', 'gy', 'gz')), may hold values from -6 to 6
- species: int32 [262144], P(('gx', 'gy', 'gz')), may hold values from 0 to 3
- cotangent: float32 [262144], P(('gx', 'gy', 'gz')), may hold values from -6 to 6
Outputs:
- energy: float32 [262144], P(('gx', 'gy', 'gz'))
- feature_grad: float32 [262144, 128], P(('gx', 'gy', 'gz'))
- up_grad: float32 [128, 128], replicated
- radial_grad: float32 [8, 384], replicated
- out_grad: float32 [384, 128], replicated
- read_grad: float32 [4, 128], replicated
Inputs may be any that keep to these rules, and one draw needn't show every extreme that they name: `ghost_rows`: every entry is a local atom row of the owning device; the 256 entries of one device are distinct. `senders`: an entry below 1024 is a local atom row of the same device; an entry v of 1024 or more is window row v - 1024, always in a cell (p, q, r) with p, q or r equal to 0 or 3. In each atom's column the live slots come first; every atom has 16 to 32 of them, and local atom 0 of every device has all 32.
All inputs are finite; a program needn't handle non-finite values.
Results may differ from a plain program's by a relative error of at most 0.0072.
Values may be sent and summed in bfloat16 or wider, within the bound.
A program may use at most 128 MiB of HBM per device.

v0:
```python
import math

import jax
import jax.numpy as jnp
import numpy as np
from jax import lax
from jax.sharding import PartitionSpec as P

DEGREE_OF = np.array([0, 1, 1, 1, 2, 2, 2, 2, 2])
HIGHEST = lax.Precision.HIGHEST


def extended(block, sides, width):
    for axis, dim in sides:
        count = lax.axis_size(axis)
        forward = [(i, i + 1) for i in range(count - 1)]
        forward.append((count - 1, 0))
        backward = [(target, source) for source, target in forward]
        low = lax.ppermute(
            lax.slice_in_dim(block, block.shape[dim] - width, None, axis=dim), axis, forward
        )
        high = lax.ppermute(lax.slice_in_dim(block, 0, width, axis=dim), axis, backward)
        block = jnp.concatenate([low, block, high], axis=dim)
    return block


def atom_block(
    lookup,
    send_rows,
    live_rows,
    harm_rows,
    radial_rows,
    species_rows,
    cot_rows,
    feature_rows,
    radial_weight,
    out_weight,
    read_weight,
):
    channels = lookup.shape[1]
    norm_factor = 1.0 / math.sqrt(send_rows.shape[0])
    basis_count = radial_rows.shape[0]
    gathered = jnp.take(lookup, send_rows, axis=0)
    coupling = (
        live_rows.astype(jnp.float32)[None, None]
        * harm_rows.astype(jnp.float32)[:, None]
        * radial_rows.astype(jnp.float32)[None]
    ).astype(jnp.bfloat16)
    mixed_sums = jnp.einsum(
        "pnka,kac->pnac", coupling, gathered, preferred_element_type=jnp.float32
    )
    radial_sel = jnp.transpose(
        radial_weight.astype(jnp.float32).reshape(basis_count, 3, channels)[:, DEGREE_OF], (1, 0, 2)
    )
    amplitude = jnp.sum(mixed_sums * radial_sel[:, :, None, :], axis=1) * norm_factor
    invariants = jnp.concatenate(
        [
            amplitude[0],
            jnp.sum(amplitude[1:4] * amplitude[1:4], axis=0),
            jnp.sum(amplitude[4:] * amplitude[4:], axis=0),
        ],
        axis=1,
    ).astype(jnp.bfloat16)
    updated = jnp.dot(
        invariants, out_weight, preferred_element_type=jnp.float32
    ) + feature_rows.astype(jnp.float32)
    species_onehot = (
        species_rows[:, None] == jnp.arange(read_weight.shape[0], dtype=jnp.int32)[None, :]
    ).astype(jnp.float32)
    readout = jnp.dot(species_onehot, read_weight, precision=HIGHEST)
    energy = jnp.sum(updated * readout, axis=1)
    d_updated = cot_rows[:, None] * readout
    d_read = jnp.dot(species_onehot.T, cot_rows[:, None] * updated, precision=HIGHEST)
    d_rounded = d_updated.astype(jnp.bfloat16)
    d_out = jnp.dot(invariants.T, d_rounded, preferred_element_type=jnp.float32)
    d_inv = jnp.dot(d_rounded, out_weight.T, preferred_element_type=jnp.float32)
    d_amp = (
        jnp.concatenate(
            [
                d_inv[None, :, :channels],
                2.0 * amplitude[1:4] * d_inv[None, :, channels : 2 * channels],
                2.0 * amplitude[4:] * d_inv[None, :, 2 * channels :],
            ],
            axis=0,
        )
        * norm_factor
    )
    d_mixed = (d_amp[:, None] * radial_sel[:, :, None, :]).astype(jnp.bfloat16)
    d_sel = jnp.sum(mixed_sums * d_amp[:, None], axis=2)
    d_radial = jnp.stack(
        [d_sel[0], jnp.sum(d_sel[1:4], axis=0), jnp.sum(d_sel[4:], axis=0)], axis=1
    ).reshape(basis_count, 3 * channels)
    d_gathered = jnp.einsum("pnka,pnac->kac", coupling, d_mixed, preferred_element_type=jnp.float32)
    return (energy, d_updated, d_read, d_out, d_radial, d_gathered)


def device_terms(
    lookup,
    senders,
    live,
    harmonics,
    radial,
    species,
    cotangent,
    features,
    radial_weight,
    out_weight,
    read_weight,
):
    atoms = senders.shape[1]
    channels = lookup.shape[1]
    block_len = min(512, atoms)

    def advance(block_no, carried):
        energy, d_res, d_lookup, d_read, d_out, d_radial = carried
        offset = block_no * block_len

        def across(source):
            return lax.dynamic_slice_in_dim(source, offset, block_len, source.ndim - 1)

        send_rows = across(senders)
        pieces = atom_block(
            lookup,
            send_rows,
            across(live),
            across(harmonics),
            across(radial),
            across(species),
            across(cotangent),
            lax.dynamic_slice_in_dim(features, offset, block_len, 0),
            radial_weight,
            out_weight,
            read_weight,
        )
        e_part, res_part, read_part, out_part, radial_part, gathered_grad = pieces
        energy = lax.dynamic_update_slice_in_dim(energy, e_part, offset, 0)
        d_res = lax.dynamic_update_slice_in_dim(d_res, res_part, offset, 0)
        d_lookup = d_lookup.at[send_rows.reshape(-1)].add(gathered_grad.reshape(-1, channels))
        return (
            energy,
            d_res,
            d_lookup,
            d_read + read_part,
            d_out + out_part,
            d_radial + radial_part,
        )

    initial = (
        jnp.zeros((atoms,), jnp.float32),
        jnp.zeros((atoms, channels), jnp.float32),
        jnp.zeros(lookup.shape, jnp.float32),
        jnp.zeros(read_weight.shape, jnp.float32),
        jnp.zeros(out_weight.shape, jnp.float32),
        jnp.zeros(radial_weight.shape, jnp.float32),
    )
    return lax.fori_loop(0, atoms // block_len, advance, initial)


def fold_axis(grid, axis):
    lower = lax.slice_in_dim(grid, 0, 1, axis=axis) + lax.slice_in_dim(grid, 2, 3, axis=axis)
    upper = lax.slice_in_dim(grid, 3, 4, axis=axis) + lax.slice_in_dim(grid, 5, 6, axis=axis)
    return jnp.concatenate([lower, upper], axis=axis)


def per_device(
    features,
    up_weight,
    radial_weight,
    out_weight,
    read_weight,
    ghost_rows,
    senders,
    live,
    harmonics,
    radial,
    species,
    cotangent,
):
    atoms = features.shape[0]
    channels = features.shape[1]
    capacity = ghost_rows.shape[3]
    tile_atoms = ghost_rows.reshape(-1)
    up_wide = up_weight.astype(jnp.float32)
    wide_features = features.astype(jnp.float32)
    mixed_rows = jnp.dot(features, up_weight, preferred_element_type=jnp.float32).astype(
        jnp.bfloat16
    )
    outgoing = jnp.take(features, tile_atoms, axis=0)
    window = extended(
        outgoing.reshape(2, 2, 2, capacity, channels), (("gx", 0), ("gy", 1), ("gz", 2)), 1
    )
    window_rows = window.reshape(64 * capacity, channels)
    window_mixed = jnp.dot(window_rows, up_weight, preferred_element_type=jnp.float32).astype(
        jnp.bfloat16
    )
    lookup = jnp.concatenate([mixed_rows, window_mixed], axis=0)
    energy, d_res, d_lookup, d_read, d_out, d_radial = device_terms(
        lookup,
        senders,
        live,
        harmonics,
        radial,
        species,
        cotangent,
        features,
        radial_weight,
        out_weight,
        read_weight,
    )
    total_atoms = atoms * lax.axis_size("gx") * lax.axis_size("gy") * lax.axis_size("gz")
    factor = 1.0 / math.sqrt(total_atoms)
    d_window = d_lookup[atoms:]
    d_own = d_lookup[:atoms]
    returned = jnp.dot(d_window, up_wide.T, precision=HIGHEST)
    grid_back = returned.reshape(4, 4, 4, capacity, channels)
    arrived = extended(grid_back, (("gx", 0), ("gy", 1), ("gz", 2)), 1)
    folded = fold_axis(fold_axis(fold_axis(arrived, 0), 1), 2).reshape(-1, channels)
    feature_grad = (jnp.dot(d_own, up_wide.T, precision=HIGHEST) + d_res).at[tile_atoms].add(folded)
    up_grad = jnp.dot(wide_features.T, d_own, precision=HIGHEST) + jnp.dot(
        window_rows.astype(jnp.float32).T, d_window, precision=HIGHEST
    )
    up_grad, d_radial, d_out, d_read = lax.psum(
        (up_grad, d_radial, d_out, d_read), ("gx", "gy", "gz")
    )
    return (
        energy,
        feature_grad,
        up_grad * factor,
        d_radial * factor,
        d_out * factor,
        d_read * factor,
    )


def solution(mesh):
    in_specs = (
        P(("gx", "gy", "gz"), None),
        P(),
        P(),
        P(),
        P(),
        P("gx", "gy", "gz", None),
        P(None, ("gx", "gy", "gz")),
        P(None, ("gx", "gy", "gz")),
        P(None, None, ("gx", "gy", "gz")),
        P(None, None, ("gx", "gy", "gz")),
        P(("gx", "gy", "gz")),
        P(("gx", "gy", "gz")),
    )
    out_specs = (P(("gx", "gy", "gz")), P(("gx", "gy", "gz"), None), P(), P(), P(), P())
    return jax.shard_map(
        per_device, mesh=mesh, in_specs=in_specs, out_specs=out_specs, check_vma=False
    )
```

profile of v0, /device:TPU:1, one launch (start us, length us, event | category | flops | bytes accessed | tf_op | source)
XLA Modules:
  0.0 773.0 jit_solution(9269639344386920217)
XLA Ops:
  10.7 5.2 collective-permute-start.1
  17.0 3.5 collective-permute-done
  20.6 6.3 collective-permute-start.2
  28.2 6.3 collective-permute-done.3
  35.8 3.8 collective-permute-start.5
  44.0 456.6 %while.25 = (s32[]{:T(128)}, f32[1024]{0:T(1024)}, f32[1024,128]{1,0:T(8,128)}, f32[3072,128]{1,0:T(8,128)S(1)}, f32[4,128]{1,0:T(4,128)S(1)}, /*index=5*/f32[38...) while((s32[]{:T(128)}, f32[1024]{0:T(1024)}, ...), condition=%wide.region_9.10_spmd.clone.clone, body=%wide.region_0.9_spmd.sunk.clone.clone.sunk | while | flops 805490176 | bytes 150178832 | solution.py:156
  59.4 3.7 copy.90
  63.1 4.0 convert_multiply_fusion.2
  67.1 57.4 %gather_fusion.1 = bf16[16384,128]{1,0:T(8,128)(2,1)} fusion(bf16[3072,128]{1,0:T(8,128)(2,1)S(1)} %get-tuple-element.788, s32[16384]{0:T(1024)S(1)} %copy-done.10), kind=kCustom, calls=%fused_computation.clone.clone.1 | custom fusion | bytes 8454144 | tf_op jit(solution)/shard_map/while/body/eval_jaxpr/jit(_take)/gather | solution.py:43
  124.5 16.6 %fusion.73 = (f32[9,512,128]{2,0,1:T(8,128)S(1)}, f32[512,128,9,8]{1,2,3,0:T(8,128)}) fusion(f32[9,8,128]{2,0,1:T(8,128)S(1)} %copy.88, f32[8,32,512]{1,0,2:T(8,128)} %convert_element_type.139, f32[9,32,512]{1,0,2:T(8,128)} %convert_multiply_fusion.2, bf16[32,512,128]{2,1,0:T(8,128)(2,1)} %bitcast.109, pred[32,512]{0,1:T(8,128)(4,1)S(1)} %copy-done.8), kind=kOutput, calls=%fused_computation.7.clone.1 | convolution fusion | flops 315293696 | bytes 26595328 | tf_op jit(solution)/shard_map/while/body/eval_jaxpr/pnka,kac->pnac/dot_general | solution.py:49
  148.2 2.9 maximum_multiply_fusion.2
  151.1 13.4 %fusion.77 = f32[9,8,128]{2,0,1:T(8,128)S(1)} fusion(f32[512,128,9,8]{1,2,3,0:T(8,128)} %get-tuple-element.733, f32[9,512,128]{2,0,1:T(8,128)S(1)} %maximum_multiply_fusion.2), kind=kLoop, calls=%fused_computation.8.clone.1 | loop fusion | flops 9427968 | bytes 21270528 | tf_op jit(solution)/shard_map/while/body/eval_jaxpr/reduce_sum | solution.py:89
  164.5 7.8 %fusion.76 = f32[32,512,128]{2,0,1:T(8,128)} fusion(f32[8,32,512]{1,0,2:T(8,128)} %convert_element_type.139, f32[9,32,512]{1,0,2:T(8,128)S(1)} %copy-done.1, f32[9,512,128]{2,0,1:T(8,128)S(1)} %maximum_multiply_fusion.2, f32[9,8,128]{2,0,1:T(8,128)S(1)} %copy.88), kind=kOutput, calls=%fused_computation.24.clone.1 | convolution fusion | flops 313786368 | bytes 11898880 | tf_op jit(solution)/shard_map/while/body/eval_jaxpr/pnka,pnac->kac/dot_general | solution.py:93
  172.3 11.5 %copy.97 = f32[32,512,128]{2,1,0:T(8,128)} copy(f32[32,512,128]{2,0,1:T(8,128)} %fusion.76) | data formatting | bytes 16777216 | tf_op jit(solution)/shard_map/while/body/eval_jaxpr/pnka,pnac->kac/transpose | solution.py:93
  183.9 88.2 %scatter_fusion = f32[3072,128]{1,0:T(8,128)S(1)} fusion(f32[3072,128]{1,0:T(8,128)S(1)} %get-tuple-element.760, s32[16384]{0:T(1024)S(1)} %bitcast.115, f32[16384,128]{1,0:T(8,128)} %bitcast.108), kind=kCustom, calls=%fused_computation.3.clone.clone.1 | custom fusion | flops 2097152 | bytes 25231360 | tf_op jit(solution)/shard_map/while/body/eval_jaxpr/scatter-add | solution.py:138
  287.5 3.7 copy.90
  291.2 4.0 convert_multiply_fusion.2
  295.2 57.4 %gather_fusion.1 = bf16[16384,128]{1,0:T(8,128)(2,1)} fusion(bf16[3072,128]{1,0:T(8,128)(2,1)S(1)} %get-tuple-element.788, s32[16384]{0:T(1024)S(1)} %copy-done.10), kind=kCustom, calls=%fused_computation.clone.clone.1 | custom fusion | bytes 8454144 | tf_op jit(solution)/shard_map/while/body/eval_jaxpr/jit(_take)/gather | solution.py:43
  352.6 16.6 %fusion.73 = (f32[9,512,128]{2,0,1:T(8,128)S(1)}, f32[512,128,9,8]{1,2,3,0:T(8,128)}) fusion(f32[9,8,128]{2,0,1:T(8,128)S(1)} %copy.88, f32[8,32,512]{1,0,2:T(8,128)} %convert_element_type.139, f32[9,32,512]{1,0,2:T(8,128)} %convert_multiply_fusion.2, bf16[32,512,128]{2,1,0:T(8,128)(2,1)} %bitcast.109, pred[32,512]{0,1:T(8,128)(4,1)S(1)} %copy-done.8), kind=kOutput, calls=%fused_computation.7.clone.1 | convolution fusion | flops 315293696 | bytes 26595328 | tf_op jit(solution)/shard_map/while/body/eval_jaxpr/pnka,kac->pnac/dot_general | solution.py:49
  376.3 2.9 maximum_multiply_fusion.2
  379.2 13.4 %fusion.77 = f32[9,8,128]{2,0,1:T(8,128)S(1)} fusion(f32[512,128,9,8]{1,2,3,0:T(8,128)} %get-tuple-element.733, f32[9,512,128]{2,0,1:T(8,128)S(1)} %maximum_multiply_fusion.2), kind=kLoop, calls=%fused_computation.8.clone.1 | loop fusion | flops 9427968 | bytes 21270528 | tf_op jit(solution)/shard_map/while/body/eval_jaxpr/reduce_sum | solution.py:89
  392.5 7.8 %fusion.76 = f32[32,512,128]{2,0,1:T(8,128)} fusion(f32[8,32,512]{1,0,2:T(8,128)} %convert_element_type.139, f32[9,32,512]{1,0,2:T(8,128)S(1)} %copy-done.1, f32[9,512,128]{2,0,1:T(8,128)S(1)} %maximum_multiply_fusion.2, f32[9,8,128]{2,0,1:T(8,128)S(1)} %copy.88), kind=kOutput, calls=%fused_computation.24.clone.1 | convolution fusion | flops 313786368 | bytes 11898880 | tf_op jit(solution)/shard_map/while/body/eval_jaxpr/pnka,pnac->kac/dot_general | solution.py:93
  400.4 11.5 %copy.97 = f32[32,512,128]{2,1,0:T(8,128)} copy(f32[32,512,128]{2,0,1:T(8,128)} %fusion.76) | data formatting | bytes 16777216 | tf_op jit(solution)/shard_map/while/body/eval_jaxpr/pnka,pnac->kac/transpose | solution.py:93
  411.9 88.2 %scatter_fusion = f32[3072,128]{1,0:T(8,128)S(1)} fusion(f32[3072,128]{1,0:T(8,128)S(1)} %get-tuple-element.760, s32[16384]{0:T(1024)S(1)} %bitcast.115, f32[16384,128]{1,0:T(8,128)} %bitcast.108), kind=kCustom, calls=%fused_computation.3.clone.clone.1 | custom fusion | flops 2097152 | bytes 25231360 | tf_op jit(solution)/shard_map/while/body/eval_jaxpr/scatter-add | solution.py:138
  505.6 76.9 %all-reduce = (f32[8,384]{1,0:T(8,128)S(1)}, f32[4,128]{1,0:T(4,128)S(1)}) all-reduce(f32[8,384]{1,0:T(8,128)S(1)} %get-tuple-element.913, f32[4,128]{1,0:T(4,128)S(1)} %get-tuple-element.911), channel_id=1, replica_groups=mesh['gx'=4,'gy'=4,'gz'=16] {'gx','gy','gz'}, use_global_device_ids=true, to_apply=%region_12.13 | all-reduce | flops 3584 | bytes 28672 | tf_op jit(solution)/shard_map/psum | solution.py:222
  582.6 4.1 collective-permute-start.8
  588.7 14.5 %collective-permute-done.8 = f32[6,1,4,32,128]{4,3,2,1,0:T(8,128)S(1)} collective-permute-done((f32[6,1,4,32,128]{4,3,2,1,0:T(8,128)S(1)}, f32[6,1,4,32,128]{4,3,2,1,0:T(8,128)S(1)}, u32[]{:S(2)}, u32[]{:S(2)}) %collective-permute-start.8) | collective-permute-done | bytes 393248 | tf_op jit(solution)/shard_map/ppermute | solution.py:19
  603.2 3.6 collective-permute-done.9
  606.9 2.1 pad_maximum_fusion.14
  609.1 4.8 collective-permute-start.11
  614.4 143.0 %all-reduce.4.cloned.1.call-done = (f32[128,128]{0,1:T(8,128)}, f32[384,128]{1,0:T(8,128)}) async-done(((f32[128,128]{0,1:T(8,128)}, f32[384,128]{1,0:T(8,128)}), (f32[128,128]{0,1:T(8,128)}, f32[384,128]{1,0:T(8,128)})) %all-reduce.4.cloned.1.call-update) | async-done | bytes 262160 | tf_op jit(solution)/shard_map/psum | solution.py:222
  763.2 2.1 scatter_fusion.1
  (241 shorter events, 70.3 us)
Async XLA Ops:
  7.2 750.3 %all-reduce.4.cloned.1.call-start = ((), (), s32[]{:S(2)}) async-start(), calls=%async_computation | async-start | bytes 524288 | tf_op jit(solution)/shard_map/psum | solution.py:222
  10.5 33.4 %copy-start.6 = (bf16[1024,128]{1,0:T(8,128)(2,1)S(1)}, bf16[1024,128]{1,0:T(8,128)(2,1)}, u32[]{:S(2)}) copy-start(bf16[1024,128]{1,0:T(8,128)(2,1)} %param.16) | copy-start | bytes 786436
  10.5 33.4 %copy-start.21 = (s32[32,1024]{1,0:T(8,128)S(1)}, s32[32,1024]{1,0:T(8,128)}, u32[]{:S(2)}) copy-start(s32[32,1024]{1,0:T(8,128)} %param.22) | copy-start | bytes 393220
  10.5 33.4 %copy-start.24 = (bf16[384,128]{1,0:T(8,128)(2,1)S(1)}, bf16[384,128]{1,0:T(8,128)(2,1)}, u32[]{:S(2)}) copy-start(bf16[384,128]{1,0:T(8,128)(2,1)} %param.19) | copy-start | bytes 294916
  10.6 33.4 %copy-start.28 = (bf16[8,384]{1,0:T(8,128)(2,1)S(1)}, bf16[8,384]{1,0:T(8,128)(2,1)}, u32[]{:S(2)}) copy-start(bf16[8,384]{1,0:T(8,128)(2,1)} %param.18) | copy-start | bytes 18436
  10.6 33.4 %copy-start.29 = (f32[4,128]{1,0:T(4,128)S(1)}, f32[4,128]{1,0:T(4,128)}, u32[]{:S(2)}) copy-start(f32[4,128]{1,0:T(4,128)} %param.20) | copy-start | bytes 6148
  10.6 33.3 %copy-start.30 = (s32[1024]{0:T(1024)S(1)}, s32[1024]{0:T(1024)}, u32[]{:S(2)}) copy-start(s32[1024]{0:T(1024)} %param.26) | copy-start | bytes 12292
  10.7 6.3 collective-permute-start.1
  16.0 4.6 collective-permute-start
  20.6 7.6 collective-permute-start.2
  26.9 7.6 collective-permute-start.3
  34.5 7.4 collective-permute-start.4
  35.8 6.1 collective-permute-start.5
  67.1 57.4 %copy-start.8 = (pred[32,512]{0,1:T(8,128)(4,1)S(1)}, pred[32,512]{0,1:T(8,128)(4,1)}, u32[]{:S(2)}) copy-start(pred[32,512]{0,1:T(8,128)(4,1)} %copy.93) | copy-start | bytes 49156 | tf_op jit(solution)/shard_map/while
  183.8 88.3 %copy-start.7 = (bf16[1024,128]{1,0:T(8,128)(2,1)S(1)}, bf16[1024,128]{1,0:T(8,128)(2,1)}, u32[]{:S(2)}) copy-start(bf16[1024,128]{1,0:T(8,128)(2,1)} %get-tuple-element.830) | copy-start | bytes 786436 | tf_op jit(solution)/shard_map/while
  183.8 88.3 %copy-start.22 = (s32[32,1024]{1,0:T(8,128)S(1)}, s32[32,1024]{1,0:T(8,128)}, u32[]{:S(2)}) copy-start(s32[32,1024]{1,0:T(8,128)} %get-tuple-element.859) | copy-start | bytes 393220 | tf_op jit(solution)/shard_map/while
  183.8 88.4 %copy-start.25 = (bf16[384,128]{1,0:T(8,128)(2,1)S(1)}, bf16[384,128]{1,0:T(8,128)(2,1)}, u32[]{:S(2)}) copy-start(bf16[384,128]{1,0:T(8,128)(2,1)} %get-tuple-element.885) | copy-start | bytes 294916 | tf_op jit(solution)/shard_map/while
  183.8 88.4 %copy-start.33 = (s32[9]{0:T(128)S(1)}, s32[9]{0:T(128)}, u32[]{:S(2)}) copy-start(s32[9]{0:T(128)} %get-tuple-element.933) | copy-start | bytes 112 | tf_op jit(solution)/shard_map/while
  295.2 57.4 %copy-start.8 = (pred[32,512]{0,1:T(8,128)(4,1)S(1)}, pred[32,512]{0,1:T(8,128)(4,1)}, u32[]{:S(2)}) copy-start(pred[32,512]{0,1:T(8,128)(4,1)} %copy.93) | copy-start | bytes 49156 | tf_op jit(solution)/shard_map/while
  411.9 88.3 %copy-start.7 = (bf16[1024,128]{1,0:T(8,128)(2,1)S(1)}, bf16[1024,128]{1,0:T(8,128)(2,1)}, u32[]{:S(2)}) copy-start(bf16[1024,128]{1,0:T(8,128)(2,1)} %get-tuple-element.830) | copy-start | bytes 786436 | tf_op jit(solution)/shard_map/while
  411.9 88.3 %copy-start.22 = (s32[32,1024]{1,0:T(8,128)S(1)}, s32[32,1024]{1,0:T(8,128)}, u32[]{:S(2)}) copy-start(s32[32,1024]{1,0:T(8,128)} %get-tuple-element.859) | copy-start | bytes 393220 | tf_op jit(solution)/shard_map/while
  411.9 88.4 %copy-start.25 = (bf16[384,128]{1,0:T(8,128)(2,1)S(1)}, bf16[384,128]{1,0:T(8,128)(2,1)}, u32[]{:S(2)}) copy-start(bf16[384,128]{1,0:T(8,128)(2,1)} %get-tuple-element.885) | copy-start | bytes 294916 | tf_op jit(solution)/shard_map/while
  411.9 88.4 %copy-start.33 = (s32[9]{0:T(128)S(1)}, s32[9]{0:T(128)}, u32[]{:S(2)}) copy-start(s32[9]{0:T(128)} %get-tuple-element.933) | copy-start | bytes 112 | tf_op jit(solution)/shard_map/while
  502.5 80.0 %collective-permute-start.7 = (f32[1,4,4,32,128]{4,3,2,1,0:T(8,128)}, f32[1,4,4,32,128]{4,3,2,1,0:T(8,128)S(1)}, u32[]{:S(2)}, u32[]{:S(2)}) collective-permute-start(f32[1,4,4,32,128]{4,3,2,1,0:T(8,128)} %bitcast.7), channel_id=1, source_target_pairs={{64,0},{128,64},{192,128},{0,192},{65,1},{129,65},{193,129},{1,193... | collective-permute-start | bytes 786440 | tf_op jit(solution)/shard_map/ppermute | solution.py:22
  502.9 79.6 %collective-permute-start.6 = (f32[1,4,4,32,128]{4,3,2,1,0:T(8,128)S(1)}, f32[1,4,4,32,128]{4,3,2,1,0:T(8,128)S(1)}, u32[]{:S(2)}, u32[]{:S(2)}) collective-permute-start(f32[1,4,4,32,128]{4,3,2,1,0:T(8,128)S(1)} %bitcast.127), channel_id=1, source_target_pairs={{0,64},{64,128},{128,192},{192,0},{1,65},{65,129},{129,193},{193,1... | collective-permute-start | bytes 786440 | tf_op jit(solution)/shard_map/ppermute | solution.py:19
  582.6 20.7 %collective-permute-start.8 = (f32[6,1,4,32,128]{4,3,2,1,0:T(8,128)S(1)}, f32[6,1,4,32,128]{4,3,2,1,0:T(8,128)S(1)}, u32[]{:S(2)}, u32[]{:S(2)}) collective-permute-start(f32[6,1,4,32,128]{4,3,2,1,0:T(8,128)S(1)} %get-tuple-element.581), channel_id=1, source_target_pairs={{0,16},{16,32},{32,48},{48,0},{1,17},{17,33},{33,49},{49,1},{2,18}... | collective-permute-start | bytes 1179656 | tf_op jit(solution)/shard_map/ppermute | solution.py:19
  586.7 20.2 %collective-permute-start.9 = (f32[6,1,4,32,128]{4,3,2,1,0:T(8,128)S(1)}, f32[6,1,4,32,128]{4,3,2,1,0:T(8,128)S(1)}, u32[]{:S(2)}, u32[]{:S(2)}) collective-permute-start(f32[6,1,4,32,128]{4,3,2,1,0:T(8,128)S(1)} %get-tuple-element.582), channel_id=1, source_target_pairs={{16,0},{32,16},{48,32},{0,48},{17,1},{33,17},{49,33},{1,49},{18,2}... | collective-permute-start | bytes 1179656 | tf_op jit(solution)/shard_map/ppermute | solution.py:22
  588.7 171.9 %copy-start.16 = (f32[1,4,4,32,128]{4,3,2,1,0:T(8,128)S(1)}, f32[1,4,4,32,128]{4,3,2,1,0:T(8,128)}, u32[]{:S(2)}) copy-start(f32[1,4,4,32,128]{4,3,2,1,0:T(8,128)} %copy-done.15) | copy-start | bytes 786436
  609.0 152.9 %copy-start.18 = (f32[6,1,4,32,128]{4,3,2,1,0:T(8,128)S(1)}, f32[6,1,4,32,128]{4,3,2,1,0:T(8,128)}, u32[]{:S(2)}) copy-start(f32[6,1,4,32,128]{4,3,2,1,0:T(8,128)} %copy-done.17) | copy-start | bytes 1179652
  609.0 152.9 %copy-start.20 = (f32[6,1,4,32,128]{4,3,2,1,0:T(8,128)S(1)}, f32[6,1,4,32,128]{4,3,2,1,0:T(8,128)}, u32[]{:S(2)}) copy-start(f32[6,1,4,32,128]{4,3,2,1,0:T(8,128)} %copy-done.19) | copy-start | bytes 1179652
  609.0 151.7 %collective-permute-start.10 = (f32[6,6,1,32,128]{4,3,2,1,0:T(8,128)}, f32[6,6,1,32,128]{4,3,2,1,0:T(8,128)}, u32[]{:S(2)}, u32[]{:S(2)}) collective-permute-start(f32[6,6,1,32,128]{4,3,2,1,0:T(8,128)} %get-tuple-element.579), channel_id=1, source_target_pairs={{0,1},{1,2},{2,3},{3,4},{4,5},{5,6},{6,7},{7,8},{8,9},{9,10},{10,1... | collective-permute-start | bytes 1769480 | tf_op jit(solution)/shard_map/ppermute | solution.py:19
  609.1 151.6 %collective-permute-start.11 = (f32[6,6,1,32,128]{4,3,2,1,0:T(8,128)}, f32[6,6,1,32,128]{4,3,2,1,0:T(8,128)}, u32[]{:S(2)}, u32[]{:S(2)}) collective-permute-start(f32[6,6,1,32,128]{4,3,2,1,0:T(8,128)} %get-tuple-element.580), channel_id=1, source_target_pairs={{1,0},{2,1},{3,2},{4,3},{5,4},{6,5},{7,6},{8,7},{9,8},{10,9},{11,1... | collective-permute-start | bytes 1769480 | tf_op jit(solution)/shard_map/ppermute | solution.py:22
  (33 other events, 229.0 us)
Sparse Core Ops, SparseCore 0:
  505.7 251.7 all-reduce.3
where the time goes:
time: 775 us; the launch traced here: 773 us
  other arithmetic  243 us (31%)
  local copies, waits for them, and re-layouts  175 us (23%)
  waiting for transfers between devices  174 us (22%)
  blocking collectives  76.9 us (10%)
  matrix products  60.9 us (8%)
  starting transfers between devices  27.1 us (3%)
  between operations  14.4 us (2%)
    scatter-add x2, other arithmetic, advance(): d_lookup.at[send_rows.reshape(-1)].add(gathered_grad.reshape(-1, channels))  176 us
    psum x1, waiting for transfers between devices, per_device(): lax.psum((up_grad, d_radial, d_out, d_read), ('gx', 'gy', 'gz'))  143 us
    gather x2, local copies, waits for them, and re-layouts, atom_block(): gathered = jnp.take(lookup, send_rows, axis=0)  115 us
    psum x1, blocking collectives, per_device(): lax.psum((up_grad, d_radial, d_out, d_read), ('gx', 'gy', 'gz'))  76.9 us
    dot_general x2, matrix products, atom_block(): jnp.einsum('pnka,kac->pnac', coupling, gathered, preferred_element_type=j...  33.1 us
    reduce_sum x2, other arithmetic, atom_block(): d_sel = jnp.sum(mixed_sums * d_amp[:, None], axis=2)  26.7 us
    transpose x2, local copies, waits for them, and re-layouts, atom_block(): jnp.einsum('pnka,pnac->kac', coupling, d_mixed, preferred_element_type=jn...  23 us
    ppermute x6, waiting for transfers between devices, extended(): lax.ppermute(lax.slice_in_dim(block, block.shape[dim] - width, None, axis...  20.4 us
  transfers between devices with their start and end apart: 13, of which 8 were waited for; matrix products, arithmetic and copies ran while one was open for 1% of the time, Pallas kernels for 0%

commit v1 on v0

v1 whole, which is shorter than its diff:
```python
import functools
import math

import jax
import jax.numpy as jnp
import numpy as np
from jax import lax
from jax.experimental import pallas as pl
from jax.experimental.pallas import tpu as pltpu
from jax.sharding import PartitionSpec as P

C = 128
LANES = 128
SLOTS = 32
ATOMS = 1024
BASIS = 8
PARTS = 9
WINDOW = 2048
TABLE = ATOMS + WINDOW
HALF = TABLE // 2
PER = ATOMS // LANES
EDGES = PER * SLOTS
BATCH = 4
DEGREE = (0, 1, 1, 1, 2, 2, 2, 2, 2)
F32 = jnp.float32
BF16 = jnp.bfloat16

NT = (((1,), (1,)), ((), ()))
TN = (((0,), (0,)), ((), ()))
NN = (((1,), (0,)), ((), ()))


def mm(a, b, dims):
    return lax.dot_general(a, b, dims, preferred_element_type=F32)


def turned(block):
    stacked = jnp.concatenate(
        [block[:, q * LANES : (q + 1) * LANES] for q in range(PER)], axis=0
    )
    return jnp.swapaxes(stacked, 0, 1)


def local_kernel(
    features, window, up, radial_w, out_w, read_w, senders, live, harm, radial, species, cot,
    energy_ref, d_upd_ref, d_own_ref, d_win_ref, grads_ref,
    table, low, high, half, y_t, r_t, w_ref, onehot, lhs, mixed, d_inv, inv, acc, gath, back, d_mix, rad_acc,
):
    up_v = up[...]
    def fill_table(source, count, first):
        part = mm(up_v, source, (((0,), (1,)), ((), ()))).astype(BF16)
        return part
    own = fill_table(features[...], ATOMS, 0)
    win = fill_table(window[...], WINDOW, ATOMS)
    table[0:C, 0:ATOMS] = own
    table[0:C, ATOMS:HALF] = win[:, 0 : HALF - ATOMS]
    table[C : 2 * C, :] = win[:, HALF - ATOMS :]

    send = turned(senders[...].astype(F32))
    second = (send >= HALF).astype(F32)
    within = send - second * HALF
    tens = jnp.floor(within * (1.0 / 16))
    half[...] = second
    high[...] = tens
    low[...] = within - tens * 16
    alive = live[...].astype(F32)
    for m in range(PARTS):
        y_t[m] = turned(harm[m].astype(F32) * alive)
    for n in range(BASIS):
        r_t[n] = turned(radial[n].astype(F32))

    for n in range(BASIS):
        for l in range(3):
            w_ref[n * 3 + l] = jnp.broadcast_to(
                radial_w[n : n + 1, l * C : (l + 1) * C].astype(F32), (8, C)
            )

    for q in range(PER):
        kind = jnp.swapaxes(jnp.broadcast_to(species[q : q + 1, :], (LANES, LANES)), 0, 1)
        weight = jnp.swapaxes(jnp.broadcast_to(cot[q : q + 1, :], (LANES, LANES)), 0, 1)
        readout = jnp.zeros((LANES, C), F32)
        for t in range(4):
            readout = jnp.where(kind == t, read_w[t : t + 1, :], readout)
        d_upd = weight * readout
        d_upd_ref[q * LANES : (q + 1) * LANES, :] = d_upd
        d_part = mm(d_upd.astype(BF16), out_w[...], NT)
        for l in range(3):
            d_inv[l, q * LANES : (q + 1) * LANES, :] = d_part[:, l * C : (l + 1) * C]

    acc[...] = jnp.zeros_like(acc)
    rad_acc[...] = jnp.zeros_like(rad_acc)

    sub16 = lax.broadcasted_iota(jnp.int32, (16, EDGES), 0)
    lane16 = lax.broadcasted_iota(jnp.int32, (16, EDGES), 1)
    owner = (sub16 & 7) == (lane16 >> 5)
    sub16f = sub16.astype(F32).astype(BF16)
    norm = 1.0 / math.sqrt(SLOTS)

    def step(i, carry):
        for g in range(BATCH):
            a = i * BATCH + g
            lo = jnp.broadcast_to(low[pl.ds(a, 1), :], (16, EDGES)).astype(BF16)
            hi = jnp.broadcast_to(high[pl.ds(a, 1), :], (16, EDGES)).astype(BF16)
            z = jnp.where(lo == sub16f, hi, jnp.full_like(hi, -1))
            for block in range(HALF // 16):
                onehot[block * 16 : block * 16 + 16, g * EDGES : (g + 1) * EDGES] = jnp.where(
                    z == block, jnp.ones_like(z), jnp.zeros_like(z)
                )
        for g in range(BATCH):
            a = i * BATCH + g
            cols = slice(g * EDGES, (g + 1) * EDGES)
            second = jnp.broadcast_to(half[pl.ds(a, 1), :], (C, EDGES)) > 0.5
            both = mm(table[...], onehot[:, cols], NN)
            gathered = jnp.where(second, both[C:], both[:C]).astype(BF16)
            r16 = []
            for j in range(BASIS // 2):
                r16.append(
                    jnp.concatenate(
                        [
                            jnp.broadcast_to(r_t[2 * j + k, pl.ds(a, 1), :], (8, EDGES))
                            for k in range(2)
                        ],
                        axis=0,
                    ).astype(BF16)
                )
            for m in range(PARTS):
                y16 = jnp.where(
                    owner, jnp.broadcast_to(y_t[m, pl.ds(a, 1), :], (16, EDGES)), 0.0
                ).astype(BF16)
                for j in range(BASIS // 2):
                    row = m * 64 + j * 16
                    lhs[g, row : row + 16, :] = y16 * r16[j]
            mixed[g] = mm(lhs[g], gathered, NT)
            amps = []
            for m in range(PARTS):
                total = None
                for n in range(BASIS):
                    term = mixed[g, m * 64 + n * 8 : m * 64 + n * 8 + 8, :] * w_ref[n * 3 + DEGREE[m]]
                    total = term if total is None else total + term
                amps.append(total * norm)
            inv1 = amps[1] * amps[1] + amps[2] * amps[2] + amps[3] * amps[3]
            inv2 = sum(amps[m] * amps[m] for m in range(5, 9)) + amps[4] * amps[4]
            for l, value in enumerate((amps[0], inv1, inv2)):
                inv[l, pl.ds(a, 8, stride=LANES), :] = value
            d_l = [d_inv[l, pl.ds(a, 8, stride=LANES), :] * norm for l in range(3)]
            d_amps = [d_l[0]]
            for m in range(1, PARTS):
                d_amps.append(2.0 * amps[m] * d_l[DEGREE[m]])
            for n in range(BASIS):
                for l in range(3):
                    total = None
                    for m in range(PARTS):
                        if DEGREE[m] != l:
                            continue
                        term = mixed[g, m * 64 + n * 8 : m * 64 + n * 8 + 8, :] * d_amps[m]
                        total = term if total is None else total + term
                    rad_acc[n * 3 + l] += total
            for m in range(PARTS):
                for j in range(BASIS // 2):
                    row = m * 64 + j * 16
                    d_mix[g, row : row + 16, :] = jnp.concatenate(
                        [d_amps[m] * w_ref[(2 * j + k) * 3 + DEGREE[m]] for k in range(2)], axis=0
                    ).astype(BF16)
            d_t = mm(d_mix[g], lhs[g], TN)
            back[0:C, cols] = jnp.where(second, 0.0, d_t).astype(BF16)
            back[C : 2 * C, cols] = jnp.where(second, d_t, 0.0).astype(BF16)
        acc[...] += mm(onehot[...], back[...], NT)
        return carry

    lax.fori_loop(0, LANES // BATCH, step, 0)

    d_out = jnp.zeros((3 * C, C), F32)
    read_rows = [jnp.zeros((1, C), F32) for _ in range(4)]
    for q in range(PER):
        rows = slice(q * LANES, (q + 1) * LANES)
        invariants = jnp.concatenate([inv[l, rows, :] for l in range(3)], axis=1).astype(BF16)
        updated = mm(invariants, out_w[...], NN) + features[rows, :].astype(F32)
        kind = jnp.swapaxes(jnp.broadcast_to(species[q : q + 1, :], (LANES, LANES)), 0, 1)
        weight = jnp.swapaxes(jnp.broadcast_to(cot[q : q + 1, :], (LANES, LANES)), 0, 1)
        readout = jnp.zeros((LANES, C), F32)
        for t in range(4):
            readout = jnp.where(kind == t, read_w[t : t + 1, :], readout)
            read_rows[t] = read_rows[t] + jnp.sum(
                jnp.where(kind == t, weight * updated, 0.0), axis=0, keepdims=True
            )
        energy_ref[q : q + 1, :] = jnp.sum(
            jnp.swapaxes(updated * readout, 0, 1), axis=0, keepdims=True
        )
        d_rounded = d_upd_ref[rows, :].astype(BF16)
        d_out = d_out + mm(invariants, d_rounded, TN)
    d_own = acc[0:ATOMS, 0:C]
    d_own_ref[...] = d_own
    d_win = jnp.concatenate([acc[ATOMS:HALF, 0:C], acc[:, C : 2 * C]], axis=0).astype(BF16)
    d_win_ref[...] = d_win
    up_sum = mm(features[...], d_own.astype(BF16), TN) + mm(window[...], d_win, TN)
    large = jnp.concatenate([up_sum, d_out], axis=0)
    blank = jnp.zeros((8, C), F32)
    for piece in range(16):
        if piece < 3:
            small = jnp.concatenate(
                [jnp.sum(rad_acc[n * 3 + piece], axis=0, keepdims=True) for n in range(BASIS)], axis=0
            )
        elif piece == 3:
            small = jnp.concatenate(read_rows + [jnp.zeros((4, C), F32)], axis=0)
        else:
            small = blank
        grads_ref[piece] = jnp.concatenate(
            [large[piece * 32 : piece * 32 + 32], small, blank], axis=0
        ).astype(BF16)


def local_terms(features, window, up, radial_w, out_w, read_w, senders, live, harm, radial, species, cot):
    vm = pl.BlockSpec(memory_space=pltpu.VMEM)
    return pl.pallas_call(
        local_kernel,
        out_shape=(
            jax.ShapeDtypeStruct((PER, LANES), F32),
            jax.ShapeDtypeStruct((ATOMS, C), F32),
            jax.ShapeDtypeStruct((ATOMS, C), F32),
            jax.ShapeDtypeStruct((WINDOW, C), BF16),
            jax.ShapeDtypeStruct((16, 48, C), BF16),
        ),
        in_specs=[vm] * 12,
        out_specs=(vm,) * 5,
        scratch_shapes=[
            pltpu.VMEM((2 * C, HALF), BF16),
            pltpu.VMEM((LANES, EDGES), F32),
            pltpu.VMEM((LANES, EDGES), F32),
            pltpu.VMEM((LANES, EDGES), F32),
            pltpu.VMEM((PARTS, LANES, EDGES), F32),
            pltpu.VMEM((BASIS, LANES, EDGES), F32),
            pltpu.VMEM((3 * BASIS, 8, C), F32),
            pltpu.VMEM((HALF, BATCH * EDGES), BF16),
            pltpu.VMEM((BATCH, PARTS * BASIS * 8, EDGES), BF16),
            pltpu.VMEM((BATCH, PARTS * BASIS * 8, C), F32),
            pltpu.VMEM((3, ATOMS, C), F32),
            pltpu.VMEM((3, ATOMS, C), F32),
            pltpu.VMEM((HALF, 2 * C), F32),
            pltpu.VMEM((8, 128), F32),
            pltpu.VMEM((2 * C, BATCH * EDGES), BF16),
            pltpu.VMEM((BATCH, PARTS * BASIS * 8, C), BF16),
            pltpu.VMEM((3 * BASIS, 8, C), F32),
        ],
        compiler_params=pltpu.CompilerParams(vmem_limit_bytes=48 * 1024 * 1024),
    )(features, window, up, radial_w, out_w, read_w, senders, live, harm, radial, species, cot)


AXES = ("gx", "gy", "gz")
MESH = pl.DeviceIdType.MESH
GHOST = 32
PIECES = 16
PIECE_ROWS = 48


def place():
    return {axis: lax.axis_index(axis) for axis in AXES}


def shifted(axis, by):
    me = place()
    me[axis] = lax.rem(me[axis] + by + lax.axis_size(axis), lax.axis_size(axis))
    return tuple(me[name] for name in AXES)


def remote(source, target, send, arrive, device):
    return pltpu.make_async_remote_copy(
        src_ref=source,
        dst_ref=target,
        send_sem=send,
        recv_sem=arrive,
        device_id=device,
        device_id_type=MESH,
    )


def column(row):
    return jnp.swapaxes(jnp.broadcast_to(row, (LANES, LANES)), 0, 1)


def spread_kernel(features, ghost, window, send, arrive):
    barrier = pltpu.get_barrier_semaphore()
    for axis in AXES:
        for by in (1, -1):
            pl.semaphore_signal(barrier, inc=1, device_id=shifted(axis, by), device_id_type=MESH)
    lane = lax.broadcasted_iota(jnp.int32, (LANES, LANES), 1)
    for h in range(2):
        rows = column(ghost[h : h + 1, :])
        hot = jnp.concatenate(
            [
                jnp.where(rows == lane + block * LANES, 1.0, 0.0).astype(BF16)
                for block in range(ATOMS // LANES)
            ],
            axis=1,
        )
        picked = mm(hot, features[...], NN).astype(BF16)
        for j in range(2):
            for k in range(2):
                first = (j * 2 + k) * GHOST
                window[1 + h, 1 + j, 1 + k] = picked[first : first + GHOST, :]
    pl.semaphore_wait(barrier, 6)
    inner = pl.ds(1, 2)
    plans = (
        ("gy", lambda at: window.at[inner, at, inner]),
        ("gx", lambda at: window.at[at, :, inner]),
        ("gz", lambda at: window.at[:, :, at]),
    )
    for number, (axis, view) in enumerate(plans):
        up = remote(
            view(2), view(0), send.at[2 * number], arrive.at[2 * number], shifted(axis, 1)
        )
        down = remote(
            view(1), view(3), send.at[2 * number + 1], arrive.at[2 * number + 1], shifted(axis, -1)
        )
        up.start()
        down.start()
        up.wait()
        down.wait()


def spread(features, ghost):
    vm = pl.BlockSpec(memory_space=pltpu.VMEM)
    return pl.pallas_call(
        spread_kernel,
        out_shape=jax.ShapeDtypeStruct((4, 4, 4, GHOST, C), BF16),
        in_specs=[vm] * 2,
        out_specs=vm,
        scratch_shapes=[pltpu.SemaphoreType.DMA((6,)), pltpu.SemaphoreType.DMA((6,))],
        compiler_params=pltpu.CompilerParams(
            collective_id=0, has_side_effects=True, vmem_limit_bytes=32 * 1024 * 1024
        ),
    )(features, ghost)


def plane_device(by):
    return shifted("gz", by)


def stack_device(by):
    me = place()
    wide = lax.axis_size("gy")
    count = lax.axis_size("gx") * wide
    other = lax.rem(me["gx"] * wide + me["gy"] + by, count)
    return (lax.div(other, wide), lax.rem(other, wide), me["gz"]), other


def finish_kernel(
    scale, d_win, grads, d_own, d_upd, ghost, up,
    feature_grad, up_grad, rad_grad, out_grad, read_grad,
    from_z, from_x, from_y, wide, narrow, first, second, third,
    near_send, near_arrive, send1, arrive1, send2, arrive2, send3, arrive3,
):
    me = place()
    k = me["gz"]
    s = me["gx"] * lax.axis_size("gy") + me["gy"]

    barrier = pltpu.get_barrier_semaphore()

    def greet(by, carry):
        pl.semaphore_signal(barrier, inc=1, device_id=plane_device(by), device_id_type=MESH)
        pl.semaphore_signal(barrier, inc=1, device_id=stack_device(by)[0], device_id_type=MESH)
        return carry

    lax.fori_loop(1, PIECES, greet, 0)
    pl.semaphore_wait(barrier, 2 * (PIECES - 1))

    def near(number, low_view, high_view, landing, axis):
        down = remote(
            low_view, landing.at[0], near_send.at[2 * number], near_arrive.at[2 * number],
            shifted(axis, -1),
        )
        above = remote(
            high_view, landing.at[1], near_send.at[2 * number + 1], near_arrive.at[2 * number + 1],
            shifted(axis, 1),
        )
        down.start()
        above.start()
        return down, above

    copies_z = near(0, d_win.at[:, :, 0], d_win.at[:, :, 3], from_z, "gz")

    def copy1(by):
        target = lax.rem(k + by, PIECES)
        return remote(
            grads.at[target], first.at[k], send1.at[target], arrive1.at[k], plane_device(by)
        )

    def copy2(by):
        device, other = stack_device(by)
        return remote(second.at[s], second.at[s], send2.at[other], arrive2.at[s], device)

    def copy3(by):
        target = lax.rem(k + by, PIECES)
        return remote(third.at[k], third.at[k], send3.at[target], arrive3.at[k], plane_device(by))

    def started(copy):
        def body(by, carry):
            copy(by).start()
            return carry

        lax.fori_loop(1, PIECES, body, 0)

    def settled(copy, slots, sems, mine):
        def body(by, carry):
            copy(by).wait_send()
            source = lax.rem(mine + by, PIECES)
            remote(
                slots.at[source], slots.at[source], sems.at[source], sems.at[source],
                plane_device(1),
            ).wait_recv()
            return carry

        lax.fori_loop(1, PIECES, body, 0)

    started(copy1)
    first[k] = grads[k]

    for copy in copies_z:
        copy.wait()
    wide[:, :, 0] = (d_win[:, :, 1].astype(F32) + from_z[1].astype(F32)).astype(BF16)
    wide[:, :, 1] = (d_win[:, :, 2].astype(F32) + from_z[0].astype(F32)).astype(BF16)
    copies_x = near(1, wide.at[0], wide.at[3], from_x, "gx")

    settled(copy1, first, arrive1, k)
    second[s] = sum_of(first)
    started(copy2)

    for copy in copies_x:
        copy.wait()
    narrow[0] = (wide[1].astype(F32) + from_x[1].astype(F32)).astype(BF16)
    narrow[1] = (wide[2].astype(F32) + from_x[0].astype(F32)).astype(BF16)
    copies_y = near(2, narrow.at[:, 0], narrow.at[:, 3], from_y, "gy")

    settled(copy2, second, arrive2, s)
    third[k] = sum_of(second)
    started(copy3)

    for copy in copies_y:
        copy.wait()
    atom = lax.broadcasted_iota(jnp.int32, (ATOMS, LANES), 0)
    total = d_own[...]
    for h in range(2):
        sides = (
            narrow[h, 1].astype(F32) + from_y[1, h].astype(F32),
            narrow[h, 2].astype(F32) + from_y[0, h].astype(F32),
        )
        folded = jnp.concatenate([side.reshape(2 * GHOST, C) for side in sides], axis=0).astype(BF16)
        hot = jnp.where(atom == ghost[h : h + 1, :], 1.0, 0.0).astype(BF16)
        total = total + mm(hot, folded, NN)
    feature_grad[...] = mm(total.astype(BF16), up[...], NT) + d_upd[...]

    settled(copy3, third, arrive3, k)
    for piece in range(4):
        up_grad[piece * 32 : piece * 32 + 32, :] = third[piece, 0:32].astype(F32) * scale
    for piece in range(12):
        out_grad[piece * 32 : piece * 32 + 32, :] = third[4 + piece, 0:32].astype(F32) * scale
    for l in range(3):
        rad_grad[:, l * C : (l + 1) * C] = third[l, 32:48].astype(F32)[0:8] * scale
    read_grad[...] = third[3, 32:48].astype(F32)[0:4] * scale


def sum_of(slots):
    total = slots[0].astype(F32)
    for piece in range(1, PIECES):
        total = total + slots[piece].astype(F32)
    return total.astype(BF16)


def finish(scale, d_win, grads, d_own, d_upd, ghost, up):
    vm = pl.BlockSpec(memory_space=pltpu.VMEM)
    sems = pltpu.SemaphoreType.DMA((PIECES,))
    return pl.pallas_call(
        functools.partial(finish_kernel, scale),
        out_shape=(
            jax.ShapeDtypeStruct((ATOMS, C), F32),
            jax.ShapeDtypeStruct((C, C), F32),
            jax.ShapeDtypeStruct((BASIS, 3 * C), F32),
            jax.ShapeDtypeStruct((3 * C, C), F32),
            jax.ShapeDtypeStruct((4, C), F32),
        ),
        in_specs=[vm] * 6,
        out_specs=(vm,) * 5,
        scratch_shapes=[
            pltpu.VMEM((2, 4, 4, GHOST, C), BF16),
            pltpu.VMEM((2, 4, 2, GHOST, C), BF16),
            pltpu.VMEM((2, 2, 2, GHOST, C), BF16),
            pltpu.VMEM((4, 4, 2, GHOST, C), BF16),
            pltpu.VMEM((2, 4, 2, GHOST, C), BF16),
            pltpu.VMEM((PIECES, PIECE_ROWS, C), BF16),
            pltpu.VMEM((PIECES, PIECE_ROWS, C), BF16),
            pltpu.VMEM((PIECES, PIECE_ROWS, C), BF16),
            pltpu.SemaphoreType.DMA((6,)),
            pltpu.SemaphoreType.DMA((6,)),
            sems, sems, sems, sems, sems, sems,
        ],
        compiler_params=pltpu.CompilerParams(
            collective_id=1, has_side_effects=True, vmem_limit_bytes=32 * 1024 * 1024
        ),
    )(d_win, grads, d_own, d_upd, ghost, up)


def per_device(
    features, up_weight, radial_weight, out_weight, read_weight,
    ghost_rows, senders, live, harmonics, radial, species, cotangent,
):
    ghost = ghost_rows.reshape(2, LANES)
    window = spread(features, ghost)
    energy, d_upd, d_own, d_win, grads = local_terms(
        features, window.reshape(WINDOW, C), up_weight, radial_weight, out_weight, read_weight,
        senders, live, harmonics, radial,
        species.reshape(PER, LANES), cotangent.reshape(PER, LANES),
    )
    scale = 1.0 / math.sqrt(ATOMS * lax.axis_size("gx") * lax.axis_size("gy") * lax.axis_size("gz"))
    feature_grad, up_grad, rad_grad, out_grad, read_grad = finish(
        scale, d_win.reshape(4, 4, 4, GHOST, C), grads, d_own, d_upd, ghost, up_weight
    )
    return energy.reshape(ATOMS), feature_grad, up_grad, rad_grad, out_grad, read_grad


def solution(mesh):
    whole = P(AXES)
    in_specs = (
        P(AXES, None), P(), P(), P(), P(),
        P("gx", "gy", "gz", None), P(None, AXES), P(None, AXES), P(None, None, AXES),
        P(None, None, AXES), whole, whole,
    )
    out_specs = (whole, P(AXES, None), P(), P(), P(), P())
    return jax.shard_map(
        per_device, mesh=mesh, in_specs=in_specs, out_specs=out_specs, check_vma=False
    )
```

time: 775 us -> 216 us (0.28)
  other arithmetic: 243 us -> 0 us
  Pallas kernels: 0 us -> 204 us
  waiting for transfers between devices: 174 us -> 0 us
  local copies, waits for them, and re-layouts: 175 us -> 10.9 us
  blocking collectives: 76.9 us -> 0 us
  matrix products: 60.9 us -> 0 us
  starting transfers between devices: 27.1 us -> 0 us
  between operations: 14.4 us -> 0.71 us
    pallas_call x0 -> x3, Pallas kernels: none -> 204 us  [the longest x1 152 us: local_terms(): pl.pallas_call(local_kernel, out_shape=(jax.ShapeDtypeStruct((PER, LANES)...]
    scatter-add x3 -> x0, other arithmetic: 179 us -> none  [the longest x2 176 us: advance(): d_lookup.at[send_rows.reshape(-1)].add(gathered_grad.reshape(-1, channels))]
    psum x1 -> x0, waiting for transfers between devices: 143 us -> none  [per_device(): lax.psum((up_grad, d_radial, d_out, d_read), ('gx', 'gy', 'gz'))]
    gather x7 -> x0, local copies, waits for them, and re-layouts: 118 us -> none  [the longest x2 115 us: atom_block(): gathered = jnp.take(lookup, send_rows, axis=0)]
    psum x1 -> x0, blocking collectives: 76.9 us -> none  [per_device(): lax.psum((up_grad, d_radial, d_out, d_read), ('gx', 'gy', 'gz'))]
    dot_general x20 -> x0, matrix products: 60.9 us -> none  [the longest x2 33.1 us: atom_block(): jnp.einsum('pnka,kac->pnac', coupling, gathered, preferred_element_type=j...]
    ppermute x12 -> x0, waiting for transfers between devices: 30.6 us -> none  [the longest x6 20.4 us: extended(): lax.ppermute(lax.slice_in_dim(block, block.shape[dim] - width, None, axis...]
    ppermute x12 -> x0, starting transfers between devices: 27.1 us -> none  [the longest x6 14.2 us: extended(): lax.ppermute(lax.slice_in_dim(block, 0, width, axis=dim), axis, backward)]
  transfers between devices with their start and end apart: 13 -> 0, of which waited for: 8 -> 0; matrix products, arithmetic and copies ran while one was open for 1% -> 0% of each run, Pallas kernels for 0% -> 0%
where the time goes in v1:
time: 216 us
  Pallas kernels  204 us (94%)
  local copies, waits for them, and re-layouts  10.9 us (5%)
    pallas_call x1, Pallas kernels, local_terms(): pl.pallas_call(local_kernel, out_shape=(jax.ShapeDtypeStruct((PER, LANES)...  152 us
    pallas_call x1, Pallas kernels, finish(): pl.pallas_call(functools.partial(finish_kernel, scale), out_shape=(jax.Sh...  27.8 us
    pallas_call x1, Pallas kernels, spread(): pl.pallas_call(spread_kernel, out_shape=jax.ShapeDtypeStruct((4, 4, 4, GH...  24.3 us
    unnamed x29, local copies, waits for them, and re-layouts  10.1 us

profile of v1, /device:TPU:1, one launch (start us, length us, event | category | flops | bytes accessed | tf_op | source)
XLA Modules:
  0.0 215.8 jit_solution(4888761651428924885)
XLA Ops:
  0.6 0.0 copy-start.8
  0.6 0.8 reshape.30.ghost
  1.4 0.0 copy-start
  1.4 0.9 copy-done
  2.4 0.0 copy-start.1
  2.4 0.0 copy-start.3
  2.4 0.0 copy-start.11
  2.4 24.3 %shard_map.163 = bf16[4,4,4,32,128]{4,3,2,1,0:T(8,128)(2,1)S(1)} custom-call(bf16[1024,128]{1,0:T(8,128)(2,1)S(1)} %copy-done, s32[2,128]{1,0:T(2,128)S(1)} %reshape.30.ghost), custom_call_target="tpu_custom_call" | custom-call | tf_op jit(solution)/shard_map/pallas_call | solution.py:322
  26.7 0.0 copy-done.8
  26.7 0.0 copy-done.1
  26.7 0.0 copy-done.3
  26.7 0.0 copy-done.11
  26.7 0.0 copy-start.2
  26.7 1.1 copy-done.2
  27.8 0.0 copy-start.4
  27.8 0.8 copy-done.4
  28.6 0.0 copy-start.5
  28.6 0.9 copy-done.5
  29.5 0.0 copy-start.6
  29.5 0.9 copy-done.6
  30.4 0.0 copy-start.7
  30.4 0.9 copy-done.7
  31.3 0.0 copy-start.9
  31.3 0.7 copy-done.9
  32.0 0.7 copy-done.10
  32.6 152.1 %shard_map.164 = (f32[8,128]{1,0:T(8,128)}, f32[1024,128]{1,0:T(8,128)S(1)}, f32[1024,128]{1,0:T(8,128)S(1)}, bf16[2048,128]{1,0:T(8,128)(2,1)S(1)}, bf16[16,48,128]{2,1,0:T(8,128)(2,1)S(1)}) custom-call(bf16[1024,128]{1,0:T(8,128)(2,1)S(1)} %copy-done.1, bf16[2048,128]{1,0:T(8,128)(2,1)S(1)} %bitcast.5, bf16[128,128]{1,0:T(8,128)(2,1)S(1)} %copy-done.4, ...), custom_call_target="tpu_custom_call" | custom-call | tf_op jit(solution)/shard_map/pallas_call | solution.py:214
  184.7 27.8 %shard_map.165 = (f32[1024,128]{1,0:T(8,128)S(1)}, f32[128,128]{1,0:T(8,128)S(1)}, f32[8,384]{1,0:T(8,128)S(1)}, f32[384,128]{1,0:T(8,128)S(1)}, f32[4,128]{1,0:T(4,128)S(1)}) custom-call(bf16[4,4,4,32,128]{4,3,2,1,0:T(8,128)(2,1)S(1)} %bitcast.6, bf16[16,48,128]{2,1,0:T(8,128)(2,1)S(1)} %get-tuple-element.18.grads, ...), custom_call_target="tpu_custom_call" | custom-call | tf_op jit(solution)/shard_map/pallas_call | solution.py:471
  212.5 0.8 copy.23
  213.3 0.6 copy.24
  213.9 0.6 copy.25
  214.5 0.7 copy.26
  215.2 0.6 copy.27
  (1 shorter events, 0.0 us)
Async XLA Ops:
  0.6 26.1 %copy-start.8 = (bf16[8,384]{1,0:T(8,128)(2,1)S(1)}, bf16[8,384]{1,0:T(8,128)(2,1)}, u32[]{:S(2)}) copy-start(bf16[8,384]{1,0:T(8,128)(2,1)} %radial_w.1) | copy-start | bytes 18436
  1.4 1.0 copy-start
  2.4 24.3 %copy-start.1 = (bf16[1024,128]{1,0:T(8,128)(2,1)S(1)}, bf16[1024,128]{1,0:T(8,128)(2,1)}, u32[]{:S(2)}) copy-start(bf16[1024,128]{1,0:T(8,128)(2,1)} %features.3) | copy-start | bytes 786436
  2.4 24.3 %copy-start.3 = (bf16[8,32,1024]{2,1,0:T(8,128)(2,1)S(1)}, bf16[8,32,1024]{2,1,0:T(8,128)(2,1)}, u32[]{:S(2)}) copy-start(bf16[8,32,1024]{2,1,0:T(8,128)(2,1)} %radial.1) | copy-start | bytes 1572868
  2.4 24.4 %copy-start.11 = (f32[4,128]{1,0:T(4,128)S(1)}, f32[4,128]{1,0:T(4,128)}, u32[]{:S(2)}) copy-start(f32[4,128]{1,0:T(4,128)} %read_w.1) | copy-start | bytes 6148
  26.7 1.1 copy-start.2
  27.8 0.8 copy-start.4
  28.6 0.9 copy-start.5
  29.5 0.9 copy-start.6
  30.4 0.9 copy-start.7
  31.3 0.7 copy-start.9
  32.0 0.7 copy-start.10

commit v2 on v1

--- a/solution.py
+++ b/solution.py
@@ -20,11 +20,12 @@
 HALF = TABLE // 2
 PER = ATOMS // LANES
 EDGES = PER * SLOTS
-BATCH = 4
+BATCH = 16
 DEGREE = (0, 1, 1, 1, 2, 2, 2, 2, 2)
 F32 = jnp.float32
 BF16 = jnp.bfloat16
 
+CHUNK = 256
 NT = (((1,), (1,)), ((), ()))
 TN = (((0,), (0,)), ((), ()))
 NN = (((1,), (0,)), ((), ()))
@@ -44,25 +45,25 @@
 def local_kernel(
     features, window, up, radial_w, out_w, read_w, senders, live, harm, radial, species, cot,
     energy_ref, d_upd_ref, d_own_ref, d_win_ref, grads_ref,
-    table, low, high, half, y_t, r_t, w_ref, onehot, lhs, mixed, d_inv, inv, acc, gath, back, d_mix, rad_acc,
+    table, low, high, low16, high16, half, y_t, r_t, w_ref, hot_rows, onehot, lhs, mixed, d_inv, inv, acc, gath, back, d_mix, rad_acc,
 ):
     up_v = up[...]
-    def fill_table(source, count, first):
-        part = mm(up_v, source, (((0,), (1,)), ((), ()))).astype(BF16)
-        return part
-    own = fill_table(features[...], ATOMS, 0)
-    win = fill_table(window[...], WINDOW, ATOMS)
-    table[0:C, 0:ATOMS] = own
-    table[0:C, ATOMS:HALF] = win[:, 0 : HALF - ATOMS]
-    table[C : 2 * C, :] = win[:, HALF - ATOMS :]
+    own = mm(features[...], up_v, NN).astype(BF16)
+    win = mm(window[...], up_v, NN).astype(BF16)
+    table[0:ATOMS, 0:C] = own
+    table[ATOMS:HALF, 0:C] = win[0 : HALF - ATOMS, :]
+    table[:, C : 2 * C] = win[HALF - ATOMS :, :]
 
     send = turned(senders[...].astype(F32))
     second = (send >= HALF).astype(F32)
     within = send - second * HALF
+    half[...] = second
     tens = jnp.floor(within * (1.0 / 16))
-    half[...] = second
-    high[...] = tens
-    low[...] = within - tens * 16
+    high16[...] = tens
+    low16[...] = within - tens * 16
+    hundreds = jnp.floor(send * (1.0 / LANES))
+    high[...] = hundreds
+    low[...] = send - hundreds * LANES
     alive = live[...].astype(F32)
     for m in range(PARTS):
         y_t[m] = turned(harm[m].astype(F32) * alive)
@@ -96,22 +97,34 @@
     sub16f = sub16.astype(F32).astype(BF16)
     norm = 1.0 / math.sqrt(SLOTS)
 
+    lane_b = lax.broadcasted_iota(jnp.int32, (EDGES, LANES), 1).astype(F32).astype(BF16)
+
     def step(i, carry):
         for g in range(BATCH):
             a = i * BATCH + g
-            lo = jnp.broadcast_to(low[pl.ds(a, 1), :], (16, EDGES)).astype(BF16)
-            hi = jnp.broadcast_to(high[pl.ds(a, 1), :], (16, EDGES)).astype(BF16)
+            rows = slice(g * EDGES, (g + 1) * EDGES)
+            lo = jnp.swapaxes(jnp.broadcast_to(low[pl.ds(a, 1), :], (LANES, EDGES)).astype(BF16), 0, 1)
+            hi = jnp.swapaxes(jnp.broadcast_to(high[pl.ds(a, 1), :], (LANES, EDGES)).astype(BF16), 0, 1)
+            upper = hi >= HALF // LANES
+            z = jnp.where(lo == lane_b, jnp.where(upper, hi - HALF // LANES, hi), jnp.full_like(hi, -1))
+            for block in range(HALF // LANES):
+                hot_rows[rows, block * LANES : (block + 1) * LANES] = jnp.where(
+                    z == block, jnp.ones_like(z), jnp.zeros_like(z)
+                )
+            both = mm(hot_rows[rows, :], table[...], NN)
+            gath[rows, :] = jnp.where(upper, both[:, C:].astype(BF16), both[:, :C].astype(BF16))
+        for g in range(BATCH):
+            a = i * BATCH + g
+            cols = slice(g * EDGES, (g + 1) * EDGES)
+            lo = jnp.broadcast_to(low16[pl.ds(a, 1), :], (16, EDGES)).astype(BF16)
+            hi = jnp.broadcast_to(high16[pl.ds(a, 1), :], (16, EDGES)).astype(BF16)
             z = jnp.where(lo == sub16f, hi, jnp.full_like(hi, -1))
             for block in range(HALF // 16):
-                onehot[block * 16 : block * 16 + 16, g * EDGES : (g + 1) * EDGES] = jnp.where(
+                onehot[block * 16 : block * 16 + 16, cols] = jnp.where(
                     z == block, jnp.ones_like(z), jnp.zeros_like(z)
                 )
         for g in range(BATCH):
             a = i * BATCH + g
-            cols = slice(g * EDGES, (g + 1) * EDGES)
-            second = jnp.broadcast_to(half[pl.ds(a, 1), :], (C, EDGES)) > 0.5
-            both = mm(table[...], onehot[:, cols], NN)
-            gathered = jnp.where(second, both[C:], both[:C]).astype(BF16)
             r16 = []
             for j in range(BASIS // 2):
                 r16.append(
@@ -130,7 +143,10 @@
                 for j in range(BASIS // 2):
                     row = m * 64 + j * 16
                     lhs[g, row : row + 16, :] = y16 * r16[j]
-            mixed[g] = mm(lhs[g], gathered, NT)
+        for g in range(BATCH):
+            mixed[g] = mm(lhs[g], gath[g * EDGES : (g + 1) * EDGES, :], NN)
+        for g in range(BATCH):
+            a = i * BATCH + g
             amps = []
             for m in range(PARTS):
                 total = None
@@ -161,10 +177,16 @@
                     d_mix[g, row : row + 16, :] = jnp.concatenate(
                         [d_amps[m] * w_ref[(2 * j + k) * 3 + DEGREE[m]] for k in range(2)], axis=0
                     ).astype(BF16)
+        for g in range(BATCH):
+            a = i * BATCH + g
+            cols = slice(g * EDGES, (g + 1) * EDGES)
+            second = jnp.broadcast_to(half[pl.ds(a, 1), :], (C, EDGES)) > 0.5
             d_t = mm(d_mix[g], lhs[g], TN)
             back[0:C, cols] = jnp.where(second, 0.0, d_t).astype(BF16)
             back[C : 2 * C, cols] = jnp.where(second, d_t, 0.0).astype(BF16)
-        acc[...] += mm(onehot[...], back[...], NT)
+        for first in range(0, HALF, CHUNK):
+            rows = slice(first, first + CHUNK)
+            acc[rows, :] += mm(onehot[rows, :], back[...], NT)
         return carry
 
     lax.fori_loop(0, LANES // BATCH, step, 0)
@@ -223,25 +245,28 @@
         in_specs=[vm] * 12,
         out_specs=(vm,) * 5,
         scratch_shapes=[
-            pltpu.VMEM((2 * C, HALF), BF16),
+            pltpu.VMEM((HALF, 2 * C), BF16),
+            pltpu.VMEM((LANES, EDGES), F32),
+            pltpu.VMEM((LANES, EDGES), F32),
             pltpu.VMEM((LANES, EDGES), F32),
             pltpu.VMEM((LANES, EDGES), F32),
             pltpu.VMEM((LANES, EDGES), F32),
             pltpu.VMEM((PARTS, LANES, EDGES), F32),
             pltpu.VMEM((BASIS, LANES, EDGES), F32),
             pltpu.VMEM((3 * BASIS, 8, C), F32),
+            pltpu.VMEM((BATCH * EDGES, HALF), BF16),
             pltpu.VMEM((HALF, BATCH * EDGES), BF16),
             pltpu.VMEM((BATCH, PARTS * BASIS * 8, EDGES), BF16),
             pltpu.VMEM((BATCH, PARTS * BASIS * 8, C), F32),
             pltpu.VMEM((3, ATOMS, C), F32),
             pltpu.VMEM((3, ATOMS, C), F32),
             pltpu.VMEM((HALF, 2 * C), F32),
-            pltpu.VMEM((8, 128), F32),
+            pltpu.VMEM((BATCH * EDGES, C), BF16),
             pltpu.VMEM((2 * C, BATCH * EDGES), BF16),
             pltpu.VMEM((BATCH, PARTS * BASIS * 8, C), BF16),
             pltpu.VMEM((3 * BASIS, 8, C), F32),
         ],
-        compiler_params=pltpu.CompilerParams(vmem_limit_bytes=48 * 1024 * 1024),
+        compiler_params=pltpu.CompilerParams(vmem_limit_bytes=50 * 1024 * 1024),
     )(features, window, up, radial_w, out_w, read_w, senders, live, harm, radial, species, cot)
 
 
@@ -326,7 +351,7 @@
         out_specs=vm,
         scratch_shapes=[pltpu.SemaphoreType.DMA((6,)), pltpu.SemaphoreType.DMA((6,))],
         compiler_params=pltpu.CompilerParams(
-            collective_id=0, has_side_effects=True, vmem_limit_bytes=32 * 1024 * 1024
+            collective_id=0, has_side_effects=True, vmem_limit_bytes=8 * 1024 * 1024
         ),
     )(features, ghost)
 
@@ -346,7 +371,7 @@
 def finish_kernel(
     scale, d_win, grads, d_own, d_upd, ghost, up,
     feature_grad, up_grad, rad_grad, out_grad, read_grad,
-    from_z, from_x, from_y, wide, narrow, first, second, third,
+    from_z, from_x, from_y, wide, narrow, first, second, third, hot,
     near_send, near_arrive, send1, arrive1, send2, arrive2, send3, arrive3,
 ):
     me = place()
@@ -413,6 +438,10 @@
 
     started(copy1)
     first[k] = grads[k]
+    atom = lax.broadcasted_iota(jnp.int32, (ATOMS, LANES), 0)
+    for h in range(2):
+        hot[h] = jnp.where(atom == ghost[h : h + 1, :], 1.0, 0.0).astype(BF16)
+    feature_grad[...] = mm(d_own[...].astype(BF16), up[...], NT) + d_upd[...]
 
     for copy in copies_z:
         copy.wait()
@@ -436,17 +465,14 @@
 
     for copy in copies_y:
         copy.wait()
-    atom = lax.broadcasted_iota(jnp.int32, (ATOMS, LANES), 0)
-    total = d_own[...]
     for h in range(2):
         sides = (
             narrow[h, 1].astype(F32) + from_y[1, h].astype(F32),
             narrow[h, 2].astype(F32) + from_y[0, h].astype(F32),
         )
         folded = jnp.concatenate([side.reshape(2 * GHOST, C) for side in sides], axis=0).astype(BF16)
-        hot = jnp.where(atom == ghost[h : h + 1, :], 1.0, 0.0).astype(BF16)
-        total = total + mm(hot, folded, NN)
-    feature_grad[...] = mm(total.astype(BF16), up[...], NT) + d_upd[...]
+        returned = mm(folded, up[...], NT).astype(BF16)
+        feature_grad[...] += mm(hot[h], returned, NN)
 
     settled(copy3, third, arrive3, k)
     for piece in range(4):
@@ -488,12 +514,13 @@
             pltpu.VMEM((PIECES, PIECE_ROWS, C), BF16),
             pltpu.VMEM((PIECES, PIECE_ROWS, C), BF16),
             pltpu.VMEM((PIECES, PIECE_ROWS, C), BF16),
+            pltpu.VMEM((2, ATOMS, LANES), BF16),
             pltpu.SemaphoreType.DMA((6,)),
             pltpu.SemaphoreType.DMA((6,)),
             sems, sems, sems, sems, sems, sems,
         ],
         compiler_params=pltpu.CompilerParams(
-            collective_id=1, has_side_effects=True, vmem_limit_bytes=32 * 1024 * 1024
+            collective_id=1, has_side_effects=True, vmem_limit_bytes=16 * 1024 * 1024
         ),
     )(d_win, grads, d_own, d_upd, ghost, up)
 

time: 216 us -> 149 us (0.69)
  Pallas kernels: 204 us -> 137 us
    pallas_call x1, Pallas kernels: 152 us -> 84.6 us  [local_terms(): pl.pallas_call(local_kernel, out_shape=(jax.ShapeDtypeStruct((PER, LANES)...]
where the time goes in v2:
time: 149 us; the launch traced here: 148 us
  Pallas kernels  137 us (92%)
  local copies, waits for them, and re-layouts  10.9 us (7%)
    pallas_call x1, Pallas kernels, local_terms(): pl.pallas_call(local_kernel, out_shape=(jax.ShapeDtypeStruct((PER, LANES)...  84.6 us
    pallas_call x1, Pallas kernels, finish(): pl.pallas_call(functools.partial(finish_kernel, scale), out_shape=(jax.Sh...  27.8 us
    pallas_call x1, Pallas kernels, spread(): pl.pallas_call(spread_kernel, out_shape=jax.ShapeDtypeStruct((4, 4, 4, GH...  24.3 us
    unnamed x29, local copies, waits for them, and re-layouts  10.1 us

profile of v2, /device:TPU:1, one launch (start us, length us, event | category | flops | bytes accessed | tf_op | source)
XLA Modules:
  0.0 148.3 jit_solution(14365050141896879208)
XLA Ops:
  0.6 0.0 copy-start.8
  0.6 0.8 reshape.30.ghost
  1.4 0.0 copy-start
  1.4 0.9 copy-done
  2.4 0.0 copy-start.1
  2.4 0.0 copy-start.3
  2.4 0.0 copy-start.11
  2.4 24.3 %shard_map.163 = bf16[4,4,4,32,128]{4,3,2,1,0:T(8,128)(2,1)S(1)} custom-call(bf16[1024,128]{1,0:T(8,128)(2,1)S(1)} %copy-done, s32[2,128]{1,0:T(2,128)S(1)} %reshape.30.ghost), custom_call_target="tpu_custom_call" | custom-call | tf_op jit(solution)/shard_map/pallas_call | solution.py:347
  26.7 0.0 copy-done.8
  26.7 0.0 copy-done.1
  26.7 0.0 copy-done.3
  26.7 0.0 copy-done.11
  26.7 0.0 copy-start.2
  26.7 1.1 copy-done.2
  27.8 0.0 copy-start.4
  27.8 0.8 copy-done.4
  28.6 0.0 copy-start.5
  28.6 0.9 copy-done.5
  29.5 0.0 copy-start.6
  29.5 0.9 copy-done.6
  30.4 0.0 copy-start.7
  30.4 0.9 copy-done.7
  31.3 0.0 copy-start.9
  31.3 0.7 copy-done.9
  32.0 0.7 copy-done.10
  32.6 84.6 %shard_map.164 = (f32[8,128]{1,0:T(8,128)}, f32[1024,128]{1,0:T(8,128)S(1)}, f32[1024,128]{1,0:T(8,128)S(1)}, bf16[2048,128]{1,0:T(8,128)(2,1)S(1)}, bf16[16,48,128]{2,1,0:T(8,128)(2,1)S(1)}) custom-call(bf16[1024,128]{1,0:T(8,128)(2,1)S(1)} %copy-done.1, bf16[2048,128]{1,0:T(8,128)(2,1)S(1)} %bitcast.5, bf16[128,128]{1,0:T(8,128)(2,1)S(1)} %copy-done.4, ...), custom_call_target="tpu_custom_call" | custom-call | tf_op jit(solution)/shard_map/pallas_call | solution.py:236
  117.2 27.8 %shard_map.165 = (f32[1024,128]{1,0:T(8,128)S(1)}, f32[128,128]{1,0:T(8,128)S(1)}, f32[8,384]{1,0:T(8,128)S(1)}, f32[384,128]{1,0:T(8,128)S(1)}, f32[4,128]{1,0:T(4,128)S(1)}) custom-call(bf16[4,4,4,32,128]{4,3,2,1,0:T(8,128)(2,1)S(1)} %bitcast.6, bf16[16,48,128]{2,1,0:T(8,128)(2,1)S(1)} %get-tuple-element.18.grads, ...), custom_call_target="tpu_custom_call" | custom-call | tf_op jit(solution)/shard_map/pallas_call | solution.py:497
  145.0 0.8 copy.23
  145.8 0.6 copy.24
  146.4 0.6 copy.25
  147.0 0.7 copy.26
  147.7 0.6 copy.27
  (1 shorter events, 0.0 us)
Async XLA Ops:
  0.6 26.1 %copy-start.8 = (bf16[8,384]{1,0:T(8,128)(2,1)S(1)}, bf16[8,384]{1,0:T(8,128)(2,1)}, u32[]{:S(2)}) copy-start(bf16[8,384]{1,0:T(8,128)(2,1)} %radial_w.1) | copy-start | bytes 18436
  1.4 1.0 copy-start
  2.4 24.3 %copy-start.1 = (bf16[1024,128]{1,0:T(8,128)(2,1)S(1)}, bf16[1024,128]{1,0:T(8,128)(2,1)}, u32[]{:S(2)}) copy-start(bf16[1024,128]{1,0:T(8,128)(2,1)} %features.3) | copy-start | bytes 786436
  2.4 24.3 %copy-start.3 = (bf16[8,32,1024]{2,1,0:T(8,128)(2,1)S(1)}, bf16[8,32,1024]{2,1,0:T(8,128)(2,1)}, u32[]{:S(2)}) copy-start(bf16[8,32,1024]{2,1,0:T(8,128)(2,1)} %radial.1) | copy-start | bytes 1572868
  2.4 24.4 %copy-start.11 = (f32[4,128]{1,0:T(4,128)S(1)}, f32[4,128]{1,0:T(4,128)}, u32[]{:S(2)}) copy-start(f32[4,128]{1,0:T(4,128)} %read_w.1) | copy-start | bytes 6148
  26.7 1.1 copy-start.2
  27.8 0.8 copy-start.4
  28.6 0.9 copy-start.5
  29.5 0.9 copy-start.6
  30.4 0.9 copy-start.7
  31.3 0.7 copy-start.9
  32.0 0.7 copy-start.10

commit v3 on v2

--- a/solution.py
+++ b/solution.py
@@ -16,8 +16,10 @@
 BASIS = 8
 PARTS = 9
 WINDOW = 2048
-TABLE = ATOMS + WINDOW
+INNER = tuple(p * 16 + q * 4 + r for p in (1, 2) for q in (1, 2) for r in (1, 2))
+TABLE = ATOMS + WINDOW - 32 * len(INNER)
 HALF = TABLE // 2
+OUTER = ((0, 21), (23, 25), (27, 37), (39, 41), (43, 64))
 PER = ATOMS // LANES
 EDGES = PER * SLOTS
 BATCH = 16
@@ -25,7 +27,7 @@
 F32 = jnp.float32
 BF16 = jnp.bfloat16
 
-CHUNK = 256
+CHUNK = 352
 NT = (((1,), (1,)), ((), ()))
 TN = (((0,), (0,)), ((), ()))
 NN = (((1,), (0,)), ((), ()))
@@ -45,16 +47,20 @@
 def local_kernel(
     features, window, up, radial_w, out_w, read_w, senders, live, harm, radial, species, cot,
     energy_ref, d_upd_ref, d_own_ref, d_win_ref, grads_ref,
-    table, low, high, low16, high16, half, y_t, r_t, w_ref, hot_rows, onehot, lhs, mixed, d_inv, inv, acc, gath, back, d_mix, rad_acc,
+    table, low, high, low16, high16, half, y_t, r_t, w_ref, onehot, lhs, mixed, d_inv, inv, acc, gath, back, d_mix, rad_acc,
 ):
     up_v = up[...]
     own = mm(features[...], up_v, NN).astype(BF16)
     win = mm(window[...], up_v, NN).astype(BF16)
     table[0:ATOMS, 0:C] = own
-    table[ATOMS:HALF, 0:C] = win[0 : HALF - ATOMS, :]
-    table[:, C : 2 * C] = win[HALF - ATOMS :, :]
+    outer = jnp.concatenate([win[first * 32 : last * 32] for first, last in OUTER], axis=0)
+    table[ATOMS:HALF, 0:C] = outer[0 : HALF - ATOMS, :]
+    table[:, C : 2 * C] = outer[HALF - ATOMS :, :]
 
     send = turned(senders[...].astype(F32))
+    named_row = send
+    for cell in INNER:
+        send = send - jnp.where(named_row >= ATOMS + 32 * (cell + 1), 32.0, 0.0)
     second = (send >= HALF).astype(F32)
     within = send - second * HALF
     half[...] = second
@@ -107,11 +113,14 @@
             hi = jnp.swapaxes(jnp.broadcast_to(high[pl.ds(a, 1), :], (LANES, EDGES)).astype(BF16), 0, 1)
             upper = hi >= HALF // LANES
             z = jnp.where(lo == lane_b, jnp.where(upper, hi - HALF // LANES, hi), jnp.full_like(hi, -1))
-            for block in range(HALF // LANES):
-                hot_rows[rows, block * LANES : (block + 1) * LANES] = jnp.where(
-                    z == block, jnp.ones_like(z), jnp.zeros_like(z)
-                )
-            both = mm(hot_rows[rows, :], table[...], NN)
+            named = jnp.concatenate(
+                [
+                    jnp.where(z == block, jnp.ones_like(z), jnp.zeros_like(z))
+                    for block in range(HALF // LANES)
+                ],
+                axis=1,
+            )
+            both = mm(named, table[...], NN)
             gath[rows, :] = jnp.where(upper, both[:, C:].astype(BF16), both[:, :C].astype(BF16))
         for g in range(BATCH):
             a = i * BATCH + g
@@ -212,8 +221,14 @@
         d_out = d_out + mm(invariants, d_rounded, TN)
     d_own = acc[0:ATOMS, 0:C]
     d_own_ref[...] = d_own
-    d_win = jnp.concatenate([acc[ATOMS:HALF, 0:C], acc[:, C : 2 * C]], axis=0).astype(BF16)
-    d_win_ref[...] = d_win
+    d_outer = jnp.concatenate([acc[ATOMS:HALF, 0:C], acc[:, C : 2 * C]], axis=0).astype(BF16)
+    d_win_ref[...] = jnp.zeros_like(d_win_ref)
+    done = 0
+    for first, last in OUTER:
+        count = (last - first) * 32
+        d_win_ref[first * 32 : last * 32, :] = d_outer[done : done + count]
+        done += count
+    d_win = d_win_ref[...]
     up_sum = mm(features[...], d_own.astype(BF16), TN) + mm(window[...], d_win, TN)
     large = jnp.concatenate([up_sum, d_out], axis=0)
     blank = jnp.zeros((8, C), F32)
@@ -254,7 +269,6 @@
             pltpu.VMEM((PARTS, LANES, EDGES), F32),
             pltpu.VMEM((BASIS, LANES, EDGES), F32),
             pltpu.VMEM((3 * BASIS, 8, C), F32),
-            pltpu.VMEM((BATCH * EDGES, HALF), BF16),
             pltpu.VMEM((HALF, BATCH * EDGES), BF16),
             pltpu.VMEM((BATCH, PARTS * BASIS * 8, EDGES), BF16),
             pltpu.VMEM((BATCH, PARTS * BASIS * 8, C), F32),
@@ -266,7 +280,7 @@
             pltpu.VMEM((BATCH, PARTS * BASIS * 8, C), BF16),
             pltpu.VMEM((3 * BASIS, 8, C), F32),
         ],
-        compiler_params=pltpu.CompilerParams(vmem_limit_bytes=50 * 1024 * 1024),
+        compiler_params=pltpu.CompilerParams(vmem_limit_bytes=60 * 1024 * 1024),
     )(features, window, up, radial_w, out_w, read_w, senders, live, harm, radial, species, cot)
 
 
@@ -302,14 +316,18 @@
     return jnp.swapaxes(jnp.broadcast_to(row, (LANES, LANES)), 0, 1)
 
 
-def spread_kernel(features, ghost, window, send, arrive):
+def spread_kernel(features, ghost_rows, window, ghost, send, arrive):
     barrier = pltpu.get_barrier_semaphore()
     for axis in AXES:
         for by in (1, -1):
             pl.semaphore_signal(barrier, inc=1, device_id=shifted(axis, by), device_id_type=MESH)
     lane = lax.broadcasted_iota(jnp.int32, (LANES, LANES), 1)
     for h in range(2):
-        rows = column(ghost[h : h + 1, :])
+        row = jnp.concatenate(
+            [ghost_rows[h, j, k : k + 1, :] for j in range(2) for k in range(2)], axis=1
+        )
+        ghost[h : h + 1, :] = row
+        rows = column(row)
         hot = jnp.concatenate(
             [
                 jnp.where(rows == lane + block * LANES, 1.0, 0.0).astype(BF16)
@@ -342,18 +360,24 @@
         down.wait()
 
 
-def spread(features, ghost):
+def spread(features, ghost_rows):
     vm = pl.BlockSpec(memory_space=pltpu.VMEM)
     return pl.pallas_call(
         spread_kernel,
-        out_shape=jax.ShapeDtypeStruct((4, 4, 4, GHOST, C), BF16),
+        out_shape=(
+            jax.ShapeDtypeStruct((4, 4, 4, GHOST, C), BF16),
+            jax.ShapeDtypeStruct((2, LANES), jnp.int32),
+        ),
         in_specs=[vm] * 2,
-        out_specs=vm,
+        out_specs=(vm,) * 2,
+        cost_estimate=pl.CostEstimate(
+            flops=2 * 256 * ATOMS * C, bytes_accessed=60_000_000, transcendentals=0
+        ),
         scratch_shapes=[pltpu.SemaphoreType.DMA((6,)), pltpu.SemaphoreType.DMA((6,))],
         compiler_params=pltpu.CompilerParams(
-            collective_id=0, has_side_effects=True, vmem_limit_bytes=8 * 1024 * 1024
+            collective_id=0, has_side_effects=True, vmem_limit_bytes=60 * 1024 * 1024
         ),
-    )(features, ghost)
+    )(features, ghost_rows)
 
 
 def plane_device(by):
@@ -520,7 +544,7 @@
             sems, sems, sems, sems, sems, sems,
         ],
         compiler_params=pltpu.CompilerParams(
-            collective_id=1, has_side_effects=True, vmem_limit_bytes=16 * 1024 * 1024
+            collective_id=1, has_side_effects=True, vmem_limit_bytes=60 * 1024 * 1024
         ),
     )(d_win, grads, d_own, d_upd, ghost, up)
 
@@ -529,8 +553,7 @@
     features, up_weight, radial_weight, out_weight, read_weight,
     ghost_rows, senders, live, harmonics, radial, species, cotangent,
 ):
-    ghost = ghost_rows.reshape(2, LANES)
-    window = spread(features, ghost)
+    window, ghost = spread(features, ghost_rows)
     energy, d_upd, d_own, d_win, grads = local_terms(
         features, window.reshape(WINDOW, C), up_weight, radial_weight, out_weight, read_weight,
         senders, live, harmonics, radial,

time: 149 us -> 139 us (0.933)
  local copies, waits for them, and re-layouts: 10.9 us -> 4.48 us
  Pallas kernels: 137 us -> 134 us
    pallas_call x1, Pallas kernels: 84.6 us -> 77.6 us  [local_terms(): pl.pallas_call(local_kernel, out_shape=(jax.ShapeDtypeStruct((PER, LANES)...]
    unnamed x29 -> x13, local copies, waits for them, and re-layouts: 10.1 us -> 4.48 us
    pallas_call x1, Pallas kernels: 27.8 us -> 30.2 us  [finish(): pl.pallas_call(functools.partial(finish_kernel, scale), out_shape=(jax.Sh...]
    pallas_call x1, Pallas kernels: 24.3 us -> 26.2 us  [spread(): pl.pallas_call(spread_kernel, out_shape=(jax.ShapeDtypeStruct((4, 4, 4, G...]
where the time goes in v3:
time: 139 us
  Pallas kernels  134 us (96%)
  local copies, waits for them, and re-layouts  4.48 us (3%)
    pallas_call x1, Pallas kernels, local_terms(): pl.pallas_call(local_kernel, out_shape=(jax.ShapeDtypeStruct((PER, LANES)...  77.6 us
    pallas_call x1, Pallas kernels, finish(): pl.pallas_call(functools.partial(finish_kernel, scale), out_shape=(jax.Sh...  30.2 us
    pallas_call x1, Pallas kernels, spread(): pl.pallas_call(spread_kernel, out_shape=(jax.ShapeDtypeStruct((4, 4, 4, G...  26.2 us
    unnamed x13, local copies, waits for them, and re-layouts  4.48 us

profile of v3, /device:TPU:1, one launch (start us, length us, event | category | flops | bytes accessed | tf_op | source)
XLA Modules:
  0.0 139.1 jit_solution(11386129437061533587)
XLA Ops:
  0.6 26.2 %shard_map.163 = (bf16[4,4,4,32,128]{4,3,2,1,0:T(8,128)(2,1)}, s32[2,128]{1,0:T(2,128)}) custom-call(bf16[1024,128]{1,0:T(8,128)(2,1)} %features.3, s32[2,2,2,32]{3,2,1,0:T(2,128)} %ghost_rows.1), custom_call_target="tpu_custom_call" | custom-call | flops 67108864 | bytes 60000000 | tf_op jit(solution)/shard_map/pallas_call | solution.py:365
  26.9 77.6 %shard_map.164 = (f32[8,128]{1,0:T(8,128)}, f32[1024,128]{1,0:T(8,128)}, f32[1024,128]{1,0:T(8,128)}, bf16[2048,128]{1,0:T(8,128)(2,1)}, bf16[16,48,128]{2,1,0:T(8,128)(2,1)}) custom-call(bf16[1024,128]{1,0:T(8,128)(2,1)} %features.3, bf16[2048,128]{1,0:T(8,128)(2,1)} %bitcast.6, bf16[128,128]{1,0:T(8,128)(2,1)} %up.3, bf16[8,384]{1,0:T(8,128)(2,1)} %radial_w.1, ...), custom_call_target="tpu_custom_call" | custom-call | tf_op jit(solution)/shard_map/pallas_call | solution.py:251
  104.4 30.2 %shard_map.165 = (f32[1024,128]{1,0:T(8,128)}, f32[128,128]{1,0:T(8,128)}, f32[8,384]{1,0:T(8,128)}, f32[384,128]{1,0:T(8,128)}, f32[4,128]{1,0:T(4,128)}) custom-call(bf16[4,4,4,32,128]{4,3,2,1,0:T(8,128)(2,1)} %bitcast.5, bf16[16,48,128]{2,1,0:T(8,128)(2,1)} %get-tuple-element.21.grads, f32[1024,128]{1,0:T(8,128)} %get-tuple-element.22.d_own, ...), custom_call_target="tpu_custom_call" | custom-call | tf_op jit(solution)/shard_map/pallas_call | solution.py:521
  134.6 0.0 copy-start.1
  134.6 0.0 copy-start
  134.6 1.9 %copy.23 = f32[1024,128]{1,0:T(8,128)} copy(f32[1024,128]{1,0:T(8,128)} %get-tuple-element.37) | data formatting | bytes 1048576
  136.5 0.0 copy-done.1
  136.5 0.0 copy-start.2
  136.5 0.6 copy.24
  137.2 0.1 copy-done.2
  137.2 0.6 copy.25
  137.8 0.0 copy-done
  137.8 0.0 copy-start.3
  137.8 0.7 copy.26
  138.5 0.0 copy-done.3
  138.5 0.6 copy.27
Async XLA Ops:
  134.6 1.9 %copy-start.1 = (f32[128,128]{1,0:T(8,128)S(1)}, f32[128,128]{1,0:T(8,128)}, u32[]{:S(2)}) copy-start(f32[128,128]{1,0:T(8,128)} %get-tuple-element.38) | copy-start | bytes 196612
  134.6 3.2 %copy-start = (f32[384,128]{1,0:T(8,128)S(1)}, f32[384,128]{1,0:T(8,128)}, u32[]{:S(2)}) copy-start(f32[384,128]{1,0:T(8,128)} %get-tuple-element.40) | copy-start | bytes 589828
  136.5 0.7 copy-start.2
  137.8 0.7 copy-start.3

commit v4 on v3

--- a/solution.py
+++ b/solution.py
@@ -393,9 +393,8 @@
 
 
 def finish_kernel(
-    scale, d_win, grads, d_own, d_upd, ghost, up,
-    feature_grad, up_grad, rad_grad, out_grad, read_grad,
-    from_z, from_x, from_y, wide, narrow, first, second, third, hot,
+    d_win, grads, summed, returned,
+    from_z, from_x, from_y, wide, narrow, first, second, third,
     near_send, near_arrive, send1, arrive1, send2, arrive2, send3, arrive3,
 ):
     me = place()
@@ -462,10 +461,6 @@
 
     started(copy1)
     first[k] = grads[k]
-    atom = lax.broadcasted_iota(jnp.int32, (ATOMS, LANES), 0)
-    for h in range(2):
-        hot[h] = jnp.where(atom == ghost[h : h + 1, :], 1.0, 0.0).astype(BF16)
-    feature_grad[...] = mm(d_own[...].astype(BF16), up[...], NT) + d_upd[...]
 
     for copy in copies_z:
         copy.wait()
@@ -494,11 +489,23 @@
             narrow[h, 1].astype(F32) + from_y[1, h].astype(F32),
             narrow[h, 2].astype(F32) + from_y[0, h].astype(F32),
         )
-        folded = jnp.concatenate([side.reshape(2 * GHOST, C) for side in sides], axis=0).astype(BF16)
-        returned = mm(folded, up[...], NT).astype(BF16)
-        feature_grad[...] += mm(hot[h], returned, NN)
+        for j in range(2):
+            returned[h, j] = sides[j].astype(BF16)
 
     settled(copy3, third, arrive3, k)
+    summed[...] = third[...]
+
+
+def result_kernel(
+    scale, third, returned, d_own, d_upd, ghost, up,
+    feature_grad, up_grad, rad_grad, out_grad, read_grad,
+):
+    atom = lax.broadcasted_iota(jnp.int32, (ATOMS, LANES), 0)
+    total = d_own[...]
+    for h in range(2):
+        hot = jnp.where(atom == ghost[h : h + 1, :], 1.0, 0.0).astype(BF16)
+        total = total + mm(hot, returned[h * LANES : (h + 1) * LANES, :], NN)
+    feature_grad[...] = mm(total.astype(BF16), up[...], NT) + d_upd[...]
     for piece in range(4):
         up_grad[piece * 32 : piece * 32 + 32, :] = third[piece, 0:32].astype(F32) * scale
     for piece in range(12):
@@ -508,18 +515,10 @@
     read_grad[...] = third[3, 32:48].astype(F32)[0:4] * scale
 
 
-def sum_of(slots):
-    total = slots[0].astype(F32)
-    for piece in range(1, PIECES):
-        total = total + slots[piece].astype(F32)
-    return total.astype(BF16)
-
-
-def finish(scale, d_win, grads, d_own, d_upd, ghost, up):
+def result(scale, *operands):
     vm = pl.BlockSpec(memory_space=pltpu.VMEM)
-    sems = pltpu.SemaphoreType.DMA((PIECES,))
     return pl.pallas_call(
-        functools.partial(finish_kernel, scale),
+        functools.partial(result_kernel, scale),
         out_shape=(
             jax.ShapeDtypeStruct((ATOMS, C), F32),
             jax.ShapeDtypeStruct((C, C), F32),
@@ -527,8 +526,30 @@
             jax.ShapeDtypeStruct((3 * C, C), F32),
             jax.ShapeDtypeStruct((4, C), F32),
         ),
-        in_specs=[vm] * 6,
+        in_specs=[vm] * len(operands),
         out_specs=(vm,) * 5,
+        compiler_params=pltpu.CompilerParams(vmem_limit_bytes=60 * 1024 * 1024),
+    )(*operands)
+
+
+def sum_of(slots):
+    total = slots[0].astype(F32)
+    for piece in range(1, PIECES):
+        total = total + slots[piece].astype(F32)
+    return total.astype(BF16)
+
+
+def finish(d_win, grads):
+    vm = pl.BlockSpec(memory_space=pltpu.VMEM)
+    sems = pltpu.SemaphoreType.DMA((PIECES,))
+    return pl.pallas_call(
+        finish_kernel,
+        out_shape=(
+            jax.ShapeDtypeStruct((PIECES, PIECE_ROWS, C), BF16),
+            jax.ShapeDtypeStruct((2, 2, 2, GHOST, C), BF16),
+        ),
+        in_specs=[vm] * 2,
+        out_specs=(vm,) * 2,
         scratch_shapes=[
             pltpu.VMEM((2, 4, 4, GHOST, C), BF16),
             pltpu.VMEM((2, 4, 2, GHOST, C), BF16),
@@ -538,7 +559,6 @@
             pltpu.VMEM((PIECES, PIECE_ROWS, C), BF16),
             pltpu.VMEM((PIECES, PIECE_ROWS, C), BF16),
             pltpu.VMEM((PIECES, PIECE_ROWS, C), BF16),
-            pltpu.VMEM((2, ATOMS, LANES), BF16),
             pltpu.SemaphoreType.DMA((6,)),
             pltpu.SemaphoreType.DMA((6,)),
             sems, sems, sems, sems, sems, sems,
@@ -546,7 +566,7 @@
         compiler_params=pltpu.CompilerParams(
             collective_id=1, has_side_effects=True, vmem_limit_bytes=60 * 1024 * 1024
         ),
-    )(d_win, grads, d_own, d_upd, ghost, up)
+    )(d_win, grads)
 
 
 def per_device(
@@ -560,8 +580,9 @@
         species.reshape(PER, LANES), cotangent.reshape(PER, LANES),
     )
     scale = 1.0 / math.sqrt(ATOMS * lax.axis_size("gx") * lax.axis_size("gy") * lax.axis_size("gz"))
-    feature_grad, up_grad, rad_grad, out_grad, read_grad = finish(
-        scale, d_win.reshape(4, 4, 4, GHOST, C), grads, d_own, d_upd, ghost, up_weight
+    summed, returned = finish(d_win.reshape(4, 4, 4, GHOST, C), grads)
+    feature_grad, up_grad, rad_grad, out_grad, read_grad = result(
+        scale, summed, returned.reshape(2 * LANES, C), d_own, d_upd, ghost, up_weight
     )
     return energy.reshape(ATOMS), feature_grad, up_grad, rad_grad, out_grad, read_grad
 

time: 139 us -> 137 us (0.986)
  local copies, waits for them, and re-layouts: 4.48 us -> 0 us
  Pallas kernels: 134 us -> 136 us
    unnamed x13 -> x0, local copies, waits for them, and re-layouts: 4.48 us -> none
    pallas_call x1 -> x2, Pallas kernels: 30.2 us -> 32.1 us  [the longest x1 29.5 us: finish(): pl.pallas_call(finish_kernel, out_shape=(jax.ShapeDtypeStruct((PIECES, PI...]
where the time goes in v4:
time: 137 us
  Pallas kernels  136 us (99%)
    pallas_call x1, Pallas kernels, local_terms(): pl.pallas_call(local_kernel, out_shape=(jax.ShapeDtypeStruct((PER, LANES)...  77.6 us
    pallas_call x1, Pallas kernels, finish(): pl.pallas_call(finish_kernel, out_shape=(jax.ShapeDtypeStruct((PIECES, PI...  29.5 us
    pallas_call x1, Pallas kernels, spread(): pl.pallas_call(spread_kernel, out_shape=(jax.ShapeDtypeStruct((4, 4, 4, G...  26.2 us

profile of v4, /device:TPU:1, one launch (start us, length us, event | category | flops | bytes accessed | tf_op | source)
XLA Modules:
  0.0 136.5 jit_solution(17776720367984470906)
XLA Ops:
  0.6 26.2 %shard_map.163 = (bf16[4,4,4,32,128]{4,3,2,1,0:T(8,128)(2,1)}, s32[2,128]{1,0:T(2,128)}) custom-call(bf16[1024,128]{1,0:T(8,128)(2,1)} %features.3, s32[2,2,2,32]{3,2,1,0:T(2,128)} %ghost_rows.1), custom_call_target="tpu_custom_call" | custom-call | flops 67108864 | bytes 60000000 | tf_op jit(solution)/shard_map/pallas_call | solution.py:365
  26.9 77.6 %shard_map.164 = (f32[8,128]{1,0:T(8,128)}, f32[1024,128]{1,0:T(8,128)}, f32[1024,128]{1,0:T(8,128)}, bf16[2048,128]{1,0:T(8,128)(2,1)}, bf16[16,48,128]{2,1,0:T(8,128)(2,1)}) custom-call(bf16[1024,128]{1,0:T(8,128)(2,1)} %features.3, bf16[2048,128]{1,0:T(8,128)(2,1)} %bitcast.7, bf16[128,128]{1,0:T(8,128)(2,1)} %up.3, bf16[8,384]{1,0:T(8,128)(2,1)} %radial_w.1, ...), custom_call_target="tpu_custom_call" | custom-call | tf_op jit(solution)/shard_map/pallas_call | solution.py:251
  104.4 29.5 %shard_map.165 = (bf16[16,48,128]{2,1,0:T(8,128)(2,1)}, bf16[2,2,2,32,128]{4,3,2,1,0:T(8,128)(2,1)}) custom-call(bf16[4,4,4,32,128]{4,3,2,1,0:T(8,128)(2,1)} %bitcast.6, bf16[16,48,128]{2,1,0:T(8,128)(2,1)} %get-tuple-element.23.grads), custom_call_target="tpu_custom_call" | custom-call | tf_op jit(solution)/shard_map/pallas_call | solution.py:545
  133.9 2.6 %shard_map.166 = (f32[1024,128]{1,0:T(8,128)}, f32[128,128]{1,0:T(8,128)}, f32[8,384]{1,0:T(8,128)}, f32[384,128]{1,0:T(8,128)}, f32[4,128]{1,0:T(4,128)}) custom-call(bf16[16,48,128]{2,1,0:T(8,128)(2,1)} %get-tuple-element.24.third, bf16[256,128]{1,0:T(8,128)(2,1)} %bitcast.8, f32[1024,128]{1,0:T(8,128)} %get-tuple-element.26.d_own, ...), custom_call_target="tpu_custom_call" | custom-call | tf_op jit(solution)/shard_map/pallas_call | solution.py:520
